TPU v7x, 512 devices: a whole 4x4x16 slice. The times are simulated.
512 devices in a mesh: blk: 16 (over x, y_hi, core), shard: 32 (over y_lo, z).
Axes of the slice: x: 4, y: 4 (y_hi: 2, y_lo: 2; y = y_hi * 2 + y_lo), z: 16, core: 2. Of those that a mesh axis runs over, the one named last changes fastest.
Arguments:
- hidden: bfloat16 [1024, 16384], P('shard', 'blk'), may hold values from -60 to 60
- proj_weight: bfloat16 [1024, 128], P('shard'), may hold values from -0.1875 to 0.1875
- passages: bfloat16 [4096, 128, 128], P(('blk', 'shard')), may hold values from -2.5 to 2.5
- cands: int32 [16, 32, 512, 4], P('blk', 'shard'), may hold values from 0 to 7, as said below
- counts: int32 [16, 32, 512], P('blk', 'shard'), may hold values from 0 to 4, as said below
- permitted: int32 [16, 512], P('blk'), may hold values 0 or 1
Outputs:
- best_scores: float32 [512, 128], P(('blk', 'shard'))
Inputs may be any that keep to these rules, and one draw needn't show every extreme that they name: `cands`: the 4 slots of one list name distinct passages of one device's 8. `counts`: slots at or after a list's count are padding.
All inputs are finite; a program needn't handle non-finite values. No bound on the sum of `permitted` on one device may be relied on, other than what follows from the above.
Results may differ from a plain program's by a relative error of at most 0.0003.
Values may be sent and summed in bfloat16 or wider, within the bound.
No kernel may reach another device: no remote copies, remote signals or barrier semaphores. Data moves between devices by JAX's collectives and lax.ppermute only.
A program may use at most 64 MiB of HBM per device.

v0:
```python
import jax
import jax.numpy as jnp
from jax import lax
from jax.sharding import PartitionSpec as P

DIM = 128
QT = 32
CAND = 4
K = 128


def passed_along(value, axis, steps):
    count = lax.axis_size(axis)
    pairs = [(source, (source + steps) % count) for source in range(count)]
    return lax.ppermute(value, axis, pairs)


def merged_2(value, axis, join):
    pieces = lax.all_gather(value, axis)
    head = pieces[0]
    tail = pieces[1:]
    subtotal, _ = lax.scan(lambda subtotal, slab: (join(subtotal, slab), None), head, tail)
    return subtotal


def project_rows(hidden, proj_weight):
    return lax.dot_general(
        hidden, proj_weight, (((0,), (0,)), ((), ())), preferred_element_type=jnp.float32
    )


def normalize(projected):
    squares_sum = jnp.sum(projected * projected, axis=1, keepdims=True)
    return (projected * lax.rsqrt(squares_sum + 1e-06)).astype(jnp.bfloat16)


def keep_best(earlier, incoming):
    combined = jnp.concatenate([earlier, incoming], axis=1)
    return lax.top_k(combined, earlier.shape[1])[0]


def live_slots(count_lists, allowed_lists, row_start, query_count):
    counted = lax.dynamic_slice_in_dim(count_lists, row_start, query_count, 0)
    allowed = lax.dynamic_slice_in_dim(allowed_lists, row_start, query_count, 0)
    slot_index = jnp.arange(CAND, dtype=jnp.int32)[None, :]
    return (slot_index < counted[:, None]) & (allowed[:, None] == 1)


def score_lists(queries, passage_stock, slot_lists, live_mask):
    query_count = queries.shape[0]
    stock_count = passage_stock.shape[0]
    flattened = queries.reshape(query_count * QT, DIM)
    similarity = jnp.einsum(
        "rd,ptd->rpt", flattened, passage_stock, preferred_element_type=jnp.float32
    )
    best_table = jnp.sum(jnp.max(similarity, axis=2).reshape(query_count, QT, stock_count), axis=1)
    matches = slot_lists[:, :, None] == jnp.arange(stock_count, dtype=jnp.int32)[None, None, :]
    scores = jnp.sum(jnp.where(matches, best_table[:, None, :], 0.0), axis=2)
    return jnp.where(live_mask, scores, 0.0)


def body(hidden, proj_weight, passages, cands, counts, permitted):
    group_count = lax.axis_size("blk")
    home_group = lax.axis_index("blk")
    lane_count = lax.axis_size("shard")
    lane_index = lax.axis_index("shard")
    token_rows = hidden.shape[1]
    group_queries = token_rows // QT
    own_queries = group_queries // lane_count
    projected = lax.psum(project_rows(hidden, proj_weight), "shard")
    query_rows = normalize(projected)
    queries = query_rows.reshape(group_queries, QT, DIM)
    slot_table = cands.reshape(cands.shape[2], cands.shape[3])
    count_table = counts.reshape(counts.shape[2])
    allowed_table = permitted.reshape(permitted.shape[1])
    best_lists = jnp.zeros((group_queries, K), jnp.float32)

    def visit(step_index, state):
        query_block, best_lists = state
        anchor = (home_group - step_index) % group_count
        row_start = anchor * group_queries
        slot_lists = lax.dynamic_slice_in_dim(slot_table, row_start, group_queries, 0)
        live_mask = live_slots(count_table, allowed_table, row_start, group_queries)
        entries = score_lists(query_block, passages, slot_lists, live_mask)
        best_lists = keep_best(best_lists, entries)
        query_block = passed_along(query_block, "blk", 1)
        best_lists = passed_along(best_lists, "blk", 1)
        return (query_block, best_lists)

    query_block, best_lists = lax.fori_loop(0, group_count, visit, (queries, best_lists))
    merged = merged_2(best_lists, "shard", keep_best)
    return lax.dynamic_slice_in_dim(merged, lane_index * own_queries, own_queries, 0)


def solution(mesh):
    in_specs = (
        P("shard", "blk"),
        P("shard", None),
        P(("blk", "shard"), None, None),
        P("blk", "shard", None, None),
        P("blk", "shard", None),
        P("blk", None),
    )
    out_specs = P(("blk", "shard"), None)
    return jax.shard_map(body, mesh=mesh, in_specs=in_specs, out_specs=out_specs, check_vma=False)
```

profile of v0, /device:TPU:8, one launch (start us, length us, event | category | flops | bytes accessed | tf_op | source)
XLA Modules:
  0.0 708.8 jit_solution(15623578972560975492)
XLA Ops:
  9.2 261.1 %all-reduce.2.cloned.1.call-done = f32[1024,128]{1,0:T(8,128)} async-done(((f32[1024,128]{1,0:T(8,128)}), f32[1024,128]{1,0:T(8,128)}) %all-reduce.2.cloned.1.call-update) | async-done | bytes 524304 | tf_op jit(solution)/shard_map/psum | solution.py:70
  272.6 284.1 %while.27 = (s32[]{:T(128)}, bf16[32,32,128]{2,1,0:T(8,128)(2,1)S(1)}, f32[32,128]{1,0:T(8,128)S(1)}, s32[]{:T(128)}, s32[512]{0:T(512)}, /*index=5*/s32[512]{0:...) while((s32[]{:T(128)}, ...), condition=%wide.region_7.8_spmd, body=%wide.region_2.7_spmd.sunk | while | flops 269546272 | bytes 2451924 | solution.py:90
  277.9 3.8 top_k.32
  281.7 4.4 collective-permute-start.1
  286.1 4.2 collective-permute-done.1
  295.7 3.8 top_k.32
  301.8 6.4 collective-permute-done.1
  313.4 3.8 top_k.32
  319.1 6.7 collective-permute-done.1
  331.2 3.8 top_k.32
  336.9 6.7 collective-permute-done.1
  348.9 3.8 top_k.32
  354.6 6.7 collective-permute-done.1
  366.7 3.8 top_k.32
  372.4 6.7 collective-permute-done.1
  390.1 6.7 collective-permute-done.1
  402.2 3.8 top_k.32
  407.9 6.7 collective-permute-done.1
  425.6 6.7 collective-permute-done.1
  437.7 3.8 top_k.32
  443.4 6.7 collective-permute-done.1
  461.2 6.7 collective-permute-done.1
  473.2 3.8 top_k.32
  478.9 6.7 collective-permute-done.1
  496.7 6.7 collective-permute-done.1
  508.7 3.8 top_k.32
  514.4 6.7 collective-permute-done.1
  532.2 6.7 collective-permute-done.1
  544.2 3.8 top_k.32
  549.9 6.7 collective-permute-done.1
  556.7 64.2 %all-gather = f32[1024,128]{1,0:T(8,128)S(1)} all-gather(f32[32,128]{1,0:T(8,128)S(1)} %get-tuple-element.225), channel_id=2, replica_groups=mesh['blk'=16,'shard'=32] {'shard'}, dimensions={0}, use_global_device_ids=true | all-gather | bytes 540672 | tf_op jit(solution)/shard_map/all_gather | solution.py:19
  621.0 80.5 %while.28 = (s32[]{:T(128)}, f32[32,128]{1,0:T(8,128)S(1)}, f32[31,32,128]{2,1,0:T(8,128)S(1)}, s32[]{:T(128)}) while((s32[]{:T(128)}, f32[32,128]{1,0:T(8,128)S(1)}, f32[31,32,128]{2,1,0:T(8,128)S(1)}, s32[]{:T(128)}) %tuple.58), condition=%wide.region_10.11_spmd, body=%wide.region_8.10_spmd.sunk | while | flops 114690 | bytes 147513 | solution.py:22
  (369 shorter events, 217.0 us)
Async XLA Ops:
  6.5 263.8 %all-reduce.2.cloned.1.call-start = ((), (), s32[]{:S(2)}) async-start(), calls=%async_computation | async-start | bytes 1048576 | tf_op jit(solution)/shard_map/psum | solution.py:70
  272.6 17.7 %collective-permute-start = (bf16[32,32,128]{2,1,0:T(8,128)(2,1)S(1)}, bf16[32,32,128]{2,1,0:T(8,128)(2,1)S(1)}, u32[]{:S(2)}, u32[]{:S(2)}) collective-permute-start(bf16[32,32,128]{2,1,0:T(8,128)(2,1)S(1)} %copy.19), channel_id=1, source_target_pairs={{0,32},{32,64},{64,96},{96,128},{128,160},{160,192},{192,224},{224... | collective-permute-start | bytes 786440 | tf_op jit(solution)/shard_map/while/body/eval_jaxpr/ppermute | solution.py:15
  281.7 8.7 %collective-permute-start.1 = (f32[32,128]{1,0:T(8,128)S(1)}, f32[32,128]{1,0:T(8,128)S(1)}, u32[]{:S(2)}, u32[]{:S(2)}) collective-permute-start(f32[32,128]{1,0:T(8,128)S(1)} %top_k.33), channel_id=1, source_target_pairs={{0,32},{32,64},{64,96},{96,128},{128,160},{160,192},{192,224},{224... | collective-permute-start | bytes 49160 | tf_op jit(solution)/shard_map/while/body/eval_jaxpr/ppermute | solution.py:15
  290.4 17.7 %collective-permute-start = (bf16[32,32,128]{2,1,0:T(8,128)(2,1)S(1)}, bf16[32,32,128]{2,1,0:T(8,128)(2,1)S(1)}, u32[]{:S(2)}, u32[]{:S(2)}) collective-permute-start(bf16[32,32,128]{2,1,0:T(8,128)(2,1)S(1)} %copy.19), channel_id=1, source_target_pairs={{0,32},{32,64},{64,96},{96,128},{128,160},{160,192},{192,224},{224... | collective-permute-start | bytes 786440 | tf_op jit(solution)/shard_map/while/body/eval_jaxpr/ppermute | solution.py:15
  299.4 8.7 %collective-permute-start.1 = (f32[32,128]{1,0:T(8,128)S(1)}, f32[32,128]{1,0:T(8,128)S(1)}, u32[]{:S(2)}, u32[]{:S(2)}) collective-permute-start(f32[32,128]{1,0:T(8,128)S(1)} %top_k.33), channel_id=1, source_target_pairs={{0,32},{32,64},{64,96},{96,128},{128,160},{160,192},{192,224},{224... | collective-permute-start | bytes 49160 | tf_op jit(solution)/shard_map/while/body/eval_jaxpr/ppermute | solution.py:15
  308.1 17.7 %collective-permute-start = (bf16[32,32,128]{2,1,0:T(8,128)(2,1)S(1)}, bf16[32,32,128]{2,1,0:T(8,128)(2,1)S(1)}, u32[]{:S(2)}, u32[]{:S(2)}) collective-permute-start(bf16[32,32,128]{2,1,0:T(8,128)(2,1)S(1)} %copy.19), channel_id=1, source_target_pairs={{0,32},{32,64},{64,96},{96,128},{128,160},{160,192},{192,224},{224... | collective-permute-start | bytes 786440 | tf_op jit(solution)/shard_map/while/body/eval_jaxpr/ppermute | solution.py:15
  317.2 8.7 %collective-permute-start.1 = (f32[32,128]{1,0:T(8,128)S(1)}, f32[32,128]{1,0:T(8,128)S(1)}, u32[]{:S(2)}, u32[]{:S(2)}) collective-permute-start(f32[32,128]{1,0:T(8,128)S(1)} %top_k.33), channel_id=1, source_target_pairs={{0,32},{32,64},{64,96},{96,128},{128,160},{160,192},{192,224},{224... | collective-permute-start | bytes 49160 | tf_op jit(solution)/shard_map/while/body/eval_jaxpr/ppermute | solution.py:15
  325.9 17.7 %collective-permute-start = (bf16[32,32,128]{2,1,0:T(8,128)(2,1)S(1)}, bf16[32,32,128]{2,1,0:T(8,128)(2,1)S(1)}, u32[]{:S(2)}, u32[]{:S(2)}) collective-permute-start(bf16[32,32,128]{2,1,0:T(8,128)(2,1)S(1)} %copy.19), channel_id=1, source_target_pairs={{0,32},{32,64},{64,96},{96,128},{128,160},{160,192},{192,224},{224... | collective-permute-start | bytes 786440 | tf_op jit(solution)/shard_map/while/body/eval_jaxpr/ppermute | solution.py:15
  335.0 8.7 %collective-permute-start.1 = (f32[32,128]{1,0:T(8,128)S(1)}, f32[32,128]{1,0:T(8,128)S(1)}, u32[]{:S(2)}, u32[]{:S(2)}) collective-permute-start(f32[32,128]{1,0:T(8,128)S(1)} %top_k.33), channel_id=1, source_target_pairs={{0,32},{32,64},{64,96},{96,128},{128,160},{160,192},{192,224},{224... | collective-permute-start | bytes 49160 | tf_op jit(solution)/shard_map/while/body/eval_jaxpr/ppermute | solution.py:15
  343.6 17.7 %collective-permute-start = (bf16[32,32,128]{2,1,0:T(8,128)(2,1)S(1)}, bf16[32,32,128]{2,1,0:T(8,128)(2,1)S(1)}, u32[]{:S(2)}, u32[]{:S(2)}) collective-permute-start(bf16[32,32,128]{2,1,0:T(8,128)(2,1)S(1)} %copy.19), channel_id=1, source_target_pairs={{0,32},{32,64},{64,96},{96,128},{128,160},{160,192},{192,224},{224... | collective-permute-start | bytes 786440 | tf_op jit(solution)/shard_map/while/body/eval_jaxpr/ppermute | solution.py:15
  352.7 8.7 %collective-permute-start.1 = (f32[32,128]{1,0:T(8,128)S(1)}, f32[32,128]{1,0:T(8,128)S(1)}, u32[]{:S(2)}, u32[]{:S(2)}) collective-permute-start(f32[32,128]{1,0:T(8,128)S(1)} %top_k.33), channel_id=1, source_target_pairs={{0,32},{32,64},{64,96},{96,128},{128,160},{160,192},{192,224},{224... | collective-permute-start | bytes 49160 | tf_op jit(solution)/shard_map/while/body/eval_jaxpr/ppermute | solution.py:15
  361.4 17.7 %collective-permute-start = (bf16[32,32,128]{2,1,0:T(8,128)(2,1)S(1)}, bf16[32,32,128]{2,1,0:T(8,128)(2,1)S(1)}, u32[]{:S(2)}, u32[]{:S(2)}) collective-permute-start(bf16[32,32,128]{2,1,0:T(8,128)(2,1)S(1)} %copy.19), channel_id=1, source_target_pairs={{0,32},{32,64},{64,96},{96,128},{128,160},{160,192},{192,224},{224... | collective-permute-start | bytes 786440 | tf_op jit(solution)/shard_map/while/body/eval_jaxpr/ppermute | solution.py:15
  370.5 8.7 %collective-permute-start.1 = (f32[32,128]{1,0:T(8,128)S(1)}, f32[32,128]{1,0:T(8,128)S(1)}, u32[]{:S(2)}, u32[]{:S(2)}) collective-permute-start(f32[32,128]{1,0:T(8,128)S(1)} %top_k.33), channel_id=1, source_target_pairs={{0,32},{32,64},{64,96},{96,128},{128,160},{160,192},{192,224},{224... | collective-permute-start | bytes 49160 | tf_op jit(solution)/shard_map/while/body/eval_jaxpr/ppermute | solution.py:15
  379.1 17.7 %collective-permute-start = (bf16[32,32,128]{2,1,0:T(8,128)(2,1)S(1)}, bf16[32,32,128]{2,1,0:T(8,128)(2,1)S(1)}, u32[]{:S(2)}, u32[]{:S(2)}) collective-permute-start(bf16[32,32,128]{2,1,0:T(8,128)(2,1)S(1)} %copy.19), channel_id=1, source_target_pairs={{0,32},{32,64},{64,96},{96,128},{128,160},{160,192},{192,224},{224... | collective-permute-start | bytes 786440 | tf_op jit(solution)/shard_map/while/body/eval_jaxpr/ppermute | solution.py:15
  388.2 8.7 %collective-permute-start.1 = (f32[32,128]{1,0:T(8,128)S(1)}, f32[32,128]{1,0:T(8,128)S(1)}, u32[]{:S(2)}, u32[]{:S(2)}) collective-permute-start(f32[32,128]{1,0:T(8,128)S(1)} %top_k.33), channel_id=1, source_target_pairs={{0,32},{32,64},{64,96},{96,128},{128,160},{160,192},{192,224},{224... | collective-permute-start | bytes 49160 | tf_op jit(solution)/shard_map/while/body/eval_jaxpr/ppermute | solution.py:15
  396.9 17.7 %collective-permute-start = (bf16[32,32,128]{2,1,0:T(8,128)(2,1)S(1)}, bf16[32,32,128]{2,1,0:T(8,128)(2,1)S(1)}, u32[]{:S(2)}, u32[]{:S(2)}) collective-permute-start(bf16[32,32,128]{2,1,0:T(8,128)(2,1)S(1)} %copy.19), channel_id=1, source_target_pairs={{0,32},{32,64},{64,96},{96,128},{128,160},{160,192},{192,224},{224... | collective-permute-start | bytes 786440 | tf_op jit(solution)/shard_map/while/body/eval_jaxpr/ppermute | solution.py:15
  406.0 8.7 %collective-permute-start.1 = (f32[32,128]{1,0:T(8,128)S(1)}, f32[32,128]{1,0:T(8,128)S(1)}, u32[]{:S(2)}, u32[]{:S(2)}) collective-permute-start(f32[32,128]{1,0:T(8,128)S(1)} %top_k.33), channel_id=1, source_target_pairs={{0,32},{32,64},{64,96},{96,128},{128,160},{160,192},{192,224},{224... | collective-permute-start | bytes 49160 | tf_op jit(solution)/shard_map/while/body/eval_jaxpr/ppermute | solution.py:15
  414.7 17.7 %collective-permute-start = (bf16[32,32,128]{2,1,0:T(8,128)(2,1)S(1)}, bf16[32,32,128]{2,1,0:T(8,128)(2,1)S(1)}, u32[]{:S(2)}, u32[]{:S(2)}) collective-permute-start(bf16[32,32,128]{2,1,0:T(8,128)(2,1)S(1)} %copy.19), channel_id=1, source_target_pairs={{0,32},{32,64},{64,96},{96,128},{128,160},{160,192},{192,224},{224... | collective-permute-start | bytes 786440 | tf_op jit(solution)/shard_map/while/body/eval_jaxpr/ppermute | solution.py:15
  423.7 8.7 %collective-permute-start.1 = (f32[32,128]{1,0:T(8,128)S(1)}, f32[32,128]{1,0:T(8,128)S(1)}, u32[]{:S(2)}, u32[]{:S(2)}) collective-permute-start(f32[32,128]{1,0:T(8,128)S(1)} %top_k.33), channel_id=1, source_target_pairs={{0,32},{32,64},{64,96},{96,128},{128,160},{160,192},{192,224},{224... | collective-permute-start | bytes 49160 | tf_op jit(solution)/shard_map/while/body/eval_jaxpr/ppermute | solution.py:15
  432.4 17.7 %collective-permute-start = (bf16[32,32,128]{2,1,0:T(8,128)(2,1)S(1)}, bf16[32,32,128]{2,1,0:T(8,128)(2,1)S(1)}, u32[]{:S(2)}, u32[]{:S(2)}) collective-permute-start(bf16[32,32,128]{2,1,0:T(8,128)(2,1)S(1)} %copy.19), channel_id=1, source_target_pairs={{0,32},{32,64},{64,96},{96,128},{128,160},{160,192},{192,224},{224... | collective-permute-start | bytes 786440 | tf_op jit(solution)/shard_map/while/body/eval_jaxpr/ppermute | solution.py:15
  441.5 8.7 %collective-permute-start.1 = (f32[32,128]{1,0:T(8,128)S(1)}, f32[32,128]{1,0:T(8,128)S(1)}, u32[]{:S(2)}, u32[]{:S(2)}) collective-permute-start(f32[32,128]{1,0:T(8,128)S(1)} %top_k.33), channel_id=1, source_target_pairs={{0,32},{32,64},{64,96},{96,128},{128,160},{160,192},{192,224},{224... | collective-permute-start | bytes 49160 | tf_op jit(solution)/shard_map/while/body/eval_jaxpr/ppermute | solution.py:15
  450.2 17.7 %collective-permute-start = (bf16[32,32,128]{2,1,0:T(8,128)(2,1)S(1)}, bf16[32,32,128]{2,1,0:T(8,128)(2,1)S(1)}, u32[]{:S(2)}, u32[]{:S(2)}) collective-permute-start(bf16[32,32,128]{2,1,0:T(8,128)(2,1)S(1)} %copy.19), channel_id=1, source_target_pairs={{0,32},{32,64},{64,96},{96,128},{128,160},{160,192},{192,224},{224... | collective-permute-start | bytes 786440 | tf_op jit(solution)/shard_map/while/body/eval_jaxpr/ppermute | solution.py:15
  459.2 8.7 %collective-permute-start.1 = (f32[32,128]{1,0:T(8,128)S(1)}, f32[32,128]{1,0:T(8,128)S(1)}, u32[]{:S(2)}, u32[]{:S(2)}) collective-permute-start(f32[32,128]{1,0:T(8,128)S(1)} %top_k.33), channel_id=1, source_target_pairs={{0,32},{32,64},{64,96},{96,128},{128,160},{160,192},{192,224},{224... | collective-permute-start | bytes 49160 | tf_op jit(solution)/shard_map/while/body/eval_jaxpr/ppermute | solution.py:15
  467.9 17.7 %collective-permute-start = (bf16[32,32,128]{2,1,0:T(8,128)(2,1)S(1)}, bf16[32,32,128]{2,1,0:T(8,128)(2,1)S(1)}, u32[]{:S(2)}, u32[]{:S(2)}) collective-permute-start(bf16[32,32,128]{2,1,0:T(8,128)(2,1)S(1)} %copy.19), channel_id=1, source_target_pairs={{0,32},{32,64},{64,96},{96,128},{128,160},{160,192},{192,224},{224... | collective-permute-start | bytes 786440 | tf_op jit(solution)/shard_map/while/body/eval_jaxpr/ppermute | solution.py:15
  477.0 8.7 %collective-permute-start.1 = (f32[32,128]{1,0:T(8,128)S(1)}, f32[32,128]{1,0:T(8,128)S(1)}, u32[]{:S(2)}, u32[]{:S(2)}) collective-permute-start(f32[32,128]{1,0:T(8,128)S(1)} %top_k.33), channel_id=1, source_target_pairs={{0,32},{32,64},{64,96},{96,128},{128,160},{160,192},{192,224},{224... | collective-permute-start | bytes 49160 | tf_op jit(solution)/shard_map/while/body/eval_jaxpr/ppermute | solution.py:15
  485.7 17.7 %collective-permute-start = (bf16[32,32,128]{2,1,0:T(8,128)(2,1)S(1)}, bf16[32,32,128]{2,1,0:T(8,128)(2,1)S(1)}, u32[]{:S(2)}, u32[]{:S(2)}) collective-permute-start(bf16[32,32,128]{2,1,0:T(8,128)(2,1)S(1)} %copy.19), channel_id=1, source_target_pairs={{0,32},{32,64},{64,96},{96,128},{128,160},{160,192},{192,224},{224... | collective-permute-start | bytes 786440 | tf_op jit(solution)/shard_map/while/body/eval_jaxpr/ppermute | solution.py:15
  494.7 8.7 %collective-permute-start.1 = (f32[32,128]{1,0:T(8,128)S(1)}, f32[32,128]{1,0:T(8,128)S(1)}, u32[]{:S(2)}, u32[]{:S(2)}) collective-permute-start(f32[32,128]{1,0:T(8,128)S(1)} %top_k.33), channel_id=1, source_target_pairs={{0,32},{32,64},{64,96},{96,128},{128,160},{160,192},{192,224},{224... | collective-permute-start | bytes 49160 | tf_op jit(solution)/shard_map/while/body/eval_jaxpr/ppermute | solution.py:15
  503.4 17.7 %collective-permute-start = (bf16[32,32,128]{2,1,0:T(8,128)(2,1)S(1)}, bf16[32,32,128]{2,1,0:T(8,128)(2,1)S(1)}, u32[]{:S(2)}, u32[]{:S(2)}) collective-permute-start(bf16[32,32,128]{2,1,0:T(8,128)(2,1)S(1)} %copy.19), channel_id=1, source_target_pairs={{0,32},{32,64},{64,96},{96,128},{128,160},{160,192},{192,224},{224... | collective-permute-start | bytes 786440 | tf_op jit(solution)/shard_map/while/body/eval_jaxpr/ppermute | solution.py:15
  521.2 17.7 %collective-permute-start = (bf16[32,32,128]{2,1,0:T(8,128)(2,1)S(1)}, bf16[32,32,128]{2,1,0:T(8,128)(2,1)S(1)}, u32[]{:S(2)}, u32[]{:S(2)}) collective-permute-start(bf16[32,32,128]{2,1,0:T(8,128)(2,1)S(1)} %copy.19), channel_id=1, source_target_pairs={{0,32},{32,64},{64,96},{96,128},{128,160},{160,192},{192,224},{224... | collective-permute-start | bytes 786440 | tf_op jit(solution)/shard_map/while/body/eval_jaxpr/ppermute | solution.py:15
  530.3 8.7 %collective-permute-start.1 = (f32[32,128]{1,0:T(8,128)S(1)}, f32[32,128]{1,0:T(8,128)S(1)}, u32[]{:S(2)}, u32[]{:S(2)}) collective-permute-start(f32[32,128]{1,0:T(8,128)S(1)} %top_k.33), channel_id=1, source_target_pairs={{0,32},{32,64},{64,96},{96,128},{128,160},{160,192},{192,224},{224... | collective-permute-start | bytes 49160 | tf_op jit(solution)/shard_map/while/body/eval_jaxpr/ppermute | solution.py:15
  538.9 17.7 %collective-permute-start = (bf16[32,32,128]{2,1,0:T(8,128)(2,1)S(1)}, bf16[32,32,128]{2,1,0:T(8,128)(2,1)S(1)}, u32[]{:S(2)}, u32[]{:S(2)}) collective-permute-start(bf16[32,32,128]{2,1,0:T(8,128)(2,1)S(1)} %copy.19), channel_id=1, source_target_pairs={{0,32},{32,64},{64,96},{96,128},{128,160},{160,192},{192,224},{224... | collective-permute-start | bytes 786440 | tf_op jit(solution)/shard_map/while/body/eval_jaxpr/ppermute | solution.py:15
  548.0 8.7 %collective-permute-start.1 = (f32[32,128]{1,0:T(8,128)S(1)}, f32[32,128]{1,0:T(8,128)S(1)}, u32[]{:S(2)}, u32[]{:S(2)}) collective-permute-start(f32[32,128]{1,0:T(8,128)S(1)} %top_k.33), channel_id=1, source_target_pairs={{0,32},{32,64},{64,96},{96,128},{128,160},{160,192},{192,224},{224... | collective-permute-start | bytes 49160 | tf_op jit(solution)/shard_map/while/body/eval_jaxpr/ppermute | solution.py:15
  (4 other events, 11.8 us)
Sparse Core Ops, SparseCore 0:
  10.3 260.0 all-reduce.1
where the time goes:
time: 711 us; the launch traced here: 709 us
  waiting for transfers between devices  366 us (51%)
  other arithmetic  156 us (22%)
  starting transfers between devices  64.2 us (9%)
  blocking collectives  64.2 us (9%)
  local copies, waits for them, and re-layouts  29.9 us (4%)
  between operations  13.5 us (2%)
  matrix products  13.2 us (2%)
    psum x1, waiting for transfers between devices, body(): projected = lax.psum(project_rows(hidden, proj_weight), 'shard')  261 us
    top_k x47, other arithmetic, keep_best(): return lax.top_k(combined, earlier.shape[1])[0]  140 us
    ppermute x32, waiting for transfers between devices, passed_along(): return lax.ppermute(value, axis, pairs)  105 us
    all_gather x1, blocking collectives, merged_2(): pieces = lax.all_gather(value, axis)  64.2 us
    ppermute x32, starting transfers between devices, passed_along(): return lax.ppermute(value, axis, pairs)  64.1 us
  transfers between devices with their start and end apart: 33, of which 17 were waited for; matrix products, arithmetic and copies ran while one was open for 16% of the time, Pallas kernels for 0%

commit v1 on v0

v1 whole, which is shorter than its diff:
```python
import jax
import jax.numpy as jnp
from jax import lax
from jax.experimental import pallas as pl
from jax.experimental.pallas import tpu as pltpu
from jax.sharding import PartitionSpec as P

DIM = 128
HID = 1024
QT = 32
PT = 128
CAND = 4
K = 128
P_DEV = 8
GROUPS = 16
LANES = 32
QUERIES = 512
TOK = QUERIES // GROUPS * QT
HID_DEV = HID // LANES
STOCK_ROWS = P_DEV * PT
MASK_ROWS = P_DEV * QUERIES // 128
ROWS = STOCK_ROWS + MASK_ROWS
HALF = GROUPS // 2
FOLD = 128 // QT
FOLD_ROWS = HID_DEV // FOLD


def vmem():
    return pl.BlockSpec(memory_space=pltpu.VMEM)


def lane_index(shape):
    return lax.broadcasted_iota(jnp.int32, shape, 1)


def row_index(shape):
    return lax.broadcasted_iota(jnp.int32, shape, 0)


def stock_kernel(passages, cands, counts, permitted, out):
    out[0:STOCK_ROWS, :] = passages[...]
    slots = row_index((P_DEV, QUERIES))
    allowed = permitted[...] == 1
    counted = counts[...]
    live = jnp.zeros((P_DEV, QUERIES), jnp.float32)
    for j in range(CAND):
        use = jnp.where(allowed & (counted > j), cands[j : j + 1, :], -1)
        live = jnp.where(use == slots, 1.0, live)
    parts = [live[:, 128 * b : 128 * (b + 1)] for b in range(QUERIES // 128)]
    out[STOCK_ROWS:ROWS, :] = jnp.concatenate(parts, axis=0).astype(jnp.bfloat16)


def stock(passages, cands, counts, permitted):
    return pl.pallas_call(
        stock_kernel,
        out_shape=jax.ShapeDtypeStruct((ROWS, DIM), jnp.bfloat16),
        in_specs=[vmem()] * 4,
        out_specs=vmem(),
        name="stock",
    )(passages, cands, counts, permitted)


def pack_kernel(hidden, weight, out):
    weight_rows = weight[...].astype(jnp.float32)
    slot = lane_index((FOLD_ROWS, 128)) // QT
    for tile in range(TOK // 128):
        block = hidden[:, 128 * tile : 128 * (tile + 1)].astype(jnp.float32)
        bands = [block[FOLD_ROWS * c : FOLD_ROWS * (c + 1), :] for c in range(FOLD)]
        for k in range(FOLD):
            folded = bands[k]
            for c in range(FOLD):
                if c != k:
                    moved = pltpu.roll(bands[c], (QT * (c - k)) % 128, 1)
                    folded = jnp.where(slot == c, moved, folded)
            both = jnp.concatenate([folded, weight_rows], axis=0)
            out[tile * FOLD + k] = both.astype(jnp.bfloat16)


def pack(hidden, weight):
    return pl.pallas_call(
        pack_kernel,
        out_shape=jax.ShapeDtypeStruct((LANES, FOLD_ROWS + HID_DEV, 128), jnp.bfloat16),
        in_specs=[vmem()] * 2,
        out_specs=vmem(),
        name="pack",
    )(hidden, weight)


def project_kernel(packed, out):
    hidden_rows = []
    weight_rows = [[] for _ in range(FOLD)]
    for source in range(LANES):
        block = packed[source].astype(jnp.float32)
        hidden_rows.append(block[0:FOLD_ROWS])
        for c in range(FOLD):
            start = FOLD_ROWS * (1 + c)
            weight_rows[c].append(block[start : start + FOLD_ROWS])
    hidden = jnp.concatenate(hidden_rows, axis=0).astype(jnp.bfloat16)
    projected = jnp.zeros((QT, DIM), jnp.float32)
    for c in range(FOLD):
        weight = jnp.concatenate(weight_rows[c], axis=0).astype(jnp.bfloat16)
        product = lax.dot_general(
            hidden, weight, (((0,), (0,)), ((), ())), preferred_element_type=jnp.float32
        )
        projected = projected + product[QT * c : QT * (c + 1), :]
    squares = jnp.sum(projected * projected, axis=1, keepdims=True)
    rows = (projected * lax.rsqrt(squares + 1e-06)).astype(jnp.bfloat16)
    for lane in range(LANES):
        out[lane] = rows


def project(packed):
    return pl.pallas_call(
        project_kernel,
        out_shape=jax.ShapeDtypeStruct((LANES, QT, DIM), jnp.bfloat16),
        in_specs=[vmem()],
        out_specs=vmem(),
        name="project",
    )(packed)


def three_parts(value):
    first = value.astype(jnp.bfloat16)
    rest = value - first.astype(jnp.float32)
    second = rest.astype(jnp.bfloat16)
    third = (rest - second.astype(jnp.float32)).astype(jnp.bfloat16)
    return first, second, third


def score_kernel(group, queries, mine, theirs, out, turned, best, masks):
    step = pl.program_id(0)

    @pl.when(step == 0)
    def _():
        turned[...] = queries[...].astype(jnp.float32).T.astype(jnp.bfloat16)

    quarter = group[0] // FOLD
    for side, block in enumerate((mine, theirs)):
        for c in range(TOK // 256):
            part = turned[:, 256 * c : 256 * (c + 1)]
            similarity = jnp.dot(
                block[0:STOCK_ROWS, :], part, preferred_element_type=jnp.float32
            )
            top = jnp.max(similarity.reshape(P_DEV, PT, 256), axis=1)
            best[side, step, :, 256 * c : 256 * (c + 1)] = top
        mask = block[STOCK_ROWS:ROWS, :].astype(jnp.float32)
        picked = mask[0:P_DEV]
        for b in range(1, QUERIES // 128):
            picked = jnp.where(quarter == b, mask[P_DEV * b : P_DEV * (b + 1)], picked)
        masks[side, step] = picked

    @pl.when(step == HALF - 1)
    def _():
        tops = best[...].reshape(GROUPS * P_DEV, TOK)
        member = (row_index((QT, TOK)) == lane_index((QT, TOK)) // QT).astype(jnp.bfloat16)
        scores = jnp.zeros((QT, 128), jnp.float32)
        for part in three_parts(tops):
            scores = scores + lax.dot_general(
                member, part, (((1,), (1,)), ((), ())), preferred_element_type=jnp.float32
            )
        wanted = (group[0] % FOLD) * QT + row_index((QT, 128))
        chosen = (lane_index((QT, 128)) == wanted).astype(jnp.bfloat16)
        live = lax.dot_general(
            chosen,
            masks[...].reshape(128, 128).astype(jnp.bfloat16),
            (((1,), (1,)), ((), ())),
            preferred_element_type=jnp.float32,
        )
        out[...] = jnp.where(live > 0.5, scores, 0.0)


def score(group, queries, mine, theirs):
    return pl.pallas_call(
        score_kernel,
        out_shape=jax.ShapeDtypeStruct((QT, 128), jnp.float32),
        grid=(HALF,),
        in_specs=[
            pl.BlockSpec(memory_space=pltpu.SMEM),
            pl.BlockSpec((TOK, DIM), lambda i: (0, 0)),
            pl.BlockSpec((ROWS, DIM), lambda i: (i, 0)),
            pl.BlockSpec((ROWS, DIM), lambda i: (i, 0)),
        ],
        out_specs=pl.BlockSpec((QT, 128), lambda i: (0, 0)),
        scratch_shapes=[
            pltpu.VMEM((DIM, TOK), jnp.bfloat16),
            pltpu.VMEM((2, HALF, P_DEV, TOK), jnp.float32),
            pltpu.VMEM((2, HALF, P_DEV, 128), jnp.float32),
        ],
        name="score",
    )(group, queries, mine, theirs)


def split_exchange(arrays, distance):
    count = len(arrays)
    if distance < count:
        result = list(arrays)
        for i in range(count):
            if not i & distance:
                result[i] = jnp.maximum(arrays[i], arrays[i + distance])
                result[i + distance] = jnp.minimum(arrays[i], arrays[i + distance])
        return result
    rows = distance // count
    upper = (row_index((8, 128)) & rows) != 0
    result = []
    for array in arrays:
        down = pltpu.roll(array, rows, 0)
        partner = down if 2 * rows == 8 else jnp.where(upper, down, pltpu.roll(array, 8 - rows, 0))
        result.append(jnp.where(upper, jnp.minimum(array, partner), jnp.maximum(array, partner)))
    return result


def select_kernel(table, out):
    arrays = []
    for v in range(LANES // 8):
        base = table[8 * v : 8 * (v + 1), :]
        arrays.append(base)
        for k in range(1, FOLD):
            arrays.append(pltpu.roll(base, QT * k, 1))
    arrays = [jnp.maximum(array, 0.0) for array in arrays]
    count = len(arrays)
    rows = row_index((8, 128))
    lanes = lane_index((8, 128))

    def signs(bit):
        return jnp.where((lanes & bit) != 0, -1.0, 1.0)

    column_sign = signs(16)
    arrays = [array * column_sign for array in arrays]
    size = 2
    while size <= K:
        flips = []
        for i in range(count):
            if size < count:
                flips.append(-1.0 if i & size else 1.0)
            elif size < K:
                flips.append(jnp.where((rows & (size // count)) != 0, -1.0, 1.0))
            else:
                flips.append(1.0)

        def flipped(values):
            return [v if isinstance(f, float) and f == 1.0 else v * f for v, f in zip(values, flips)]

        arrays = flipped(arrays)
        distance = size // 2
        while distance:
            arrays = split_exchange(arrays, distance)
            distance //= 2
        arrays = flipped(arrays)
        size *= 2
    width = 16
    while width:
        arrays = [array * column_sign for array in arrays]
        arrays = [jnp.maximum(array, pltpu.roll(array, width, 1)) for array in arrays]
        width //= 2
        if width:
            column_sign = signs(width)
            arrays = [array * column_sign for array in arrays]
        distance = K // 2
        while distance:
            arrays = split_exchange(arrays, distance)
            distance //= 2
    total = jnp.zeros((8, 128), jnp.float32)
    for i, array in enumerate(arrays):
        total = total + jnp.where(lanes == rows * count + i, array, 0.0)
    out[...] = jnp.sum(total, axis=0, keepdims=True)


def select(table):
    return pl.pallas_call(
        select_kernel,
        out_shape=jax.ShapeDtypeStruct((1, K), jnp.float32),
        in_specs=[vmem()],
        out_specs=vmem(),
        name="select",
    )(table)


def body(hidden, proj_weight, passages, cands, counts, permitted):
    group = lax.axis_index("blk").astype(jnp.int32).reshape(1)
    slots = cands.reshape(QUERIES, CAND).T
    own = stock(
        passages.reshape(STOCK_ROWS, DIM), slots, counts.reshape(1, QUERIES), permitted
    )
    same_core = [list(range(core, GROUPS, 2)) for core in range(2)]
    mine = lax.all_gather(own, "blk", axis=0, tiled=True, axis_index_groups=same_core)
    packed = lax.all_to_all(pack(hidden, proj_weight), "shard", 0, 0, tiled=True)
    rows = project(packed)
    theirs = lax.ppermute(mine, "blk", [(i, i ^ 1) for i in range(GROUPS)])
    queries = lax.all_to_all(rows, "shard", 0, 0, tiled=True).reshape(TOK, DIM)
    table = score(group, queries, mine, theirs)
    entries = lax.all_to_all(table.reshape(LANES, 1, 128), "shard", 0, 0, tiled=True)
    return select(entries.reshape(LANES, 128))


def solution(mesh):
    in_specs = (
        P("shard", "blk"),
        P("shard", None),
        P(("blk", "shard"), None, None),
        P("blk", "shard", None, None),
        P("blk", "shard", None),
        P("blk", None),
    )
    out_specs = P(("blk", "shard"), None)
    return jax.shard_map(body, mesh=mesh, in_specs=in_specs, out_specs=out_specs, check_vma=False)
```

time: 711 us -> 168 us (0.24)
  the two profiles are of different devices: /device:TPU:8 before, /device:TPU:2 now
where the time goes in v1:
time: 168 us; the launch traced here: 167 us
  waiting for transfers between devices  83 us (49%)
  starting transfers between devices  31 us (18%)
  Pallas kernels  19.9 us (12%)
  blocking collectives  17.7 us (11%)
  between operations  13.4 us (8%)
  local copies, waits for them, and re-layouts  2.13 us (1%)
    all_gather x1, waiting for transfers between devices, body(): lax.all_gather(own, 'blk', axis=0, tiled=True, axis_index_groups=same_core)  60.2 us
    all_to_all x1, waiting for transfers between devices, body(): queries = lax.all_to_all(rows, 'shard', 0, 0, tiled=True).reshape(TOK, DIM)  22.9 us
    all_to_all x1, blocking collectives, body(): lax.all_to_all(table.reshape(LANES, 1, 128), 'shard', 0, 0, tiled=True)  17.7 us
    all_to_all x1, starting transfers between devices, body(): lax.all_to_all(pack(hidden, proj_weight), 'shard', 0, 0, tiled=True)  16.5 us
    all_to_all x1, starting transfers between devices, body(): queries = lax.all_to_all(rows, 'shard', 0, 0, tiled=True).reshape(TOK, DIM)  12.6 us
    pallas_call x1, Pallas kernels, score(): pl.pallas_call(score_kernel, out_shape=jax.ShapeDtypeStruct((QT, 128), jn...  12.4 us
  transfers between devices with their start and end apart: 4, of which 2 were waited for; matrix products, arithmetic and copies ran while one was open for 0% of the time, Pallas kernels for 2%

profile of v1, /device:TPU:2, one launch (start us, length us, event | category | flops | bytes accessed | tf_op | source)
XLA Modules:
  0.0 167.2 jit_solution(4620516116784036795)
XLA Ops:
  6.5 0.0 all-gather.2.cloned.1.call-start
  6.5 1.7 %stock.1 = bf16[1056,128]{1,0:T(8,128)(2,1)} custom-call(bf16[1024,128]{1,0:T(8,128)(2,1)} %bitcast.12, s32[4,512]{1,0:T(4,128)} %bitcast.15, s32[1,512]{1,0:T(1,128)} %bitcast.16, s32[1,512]{1,0:T(1,128)} %permitted.1), custom_call_target="tpu_custom_call" | custom-call | tf_op jit(solution)/shard_map/stock/pallas_call | solution.py:54
  8.2 0.0 all-gather.2.cloned.1.call-update
  8.3 1.7 %pack.1 = bf16[32,40,128]{2,1,0:T(8,128)(2,1)} custom-call(bf16[32,1024]{1,0:T(8,128)(2,1)} %hidden.1, bf16[32,128]{1,0:T(8,128)(2,1)} %weight.1), custom_call_target="tpu_custom_call" | custom-call | tf_op jit(solution)/shard_map/pack/pallas_call | solution.py:80
  10.0 16.5 %all-to-all-start = ((bf16[32,40,128]{2,1,0:T(8,128)(2,1)}), bf16[32,40,128]{2,1,0:T(8,128)(2,1)S(1)}, u32[]{:S(2)}, u32[]{:S(2)}) async-start(bf16[32,40,128]{2,1,0:T(8,128)(2,1)} %pack.1), calls=%async_computation | async-start | bytes 655360 | tf_op jit(solution)/shard_map/all_to_all | solution.py:286
  26.5 60.2 %all-gather.2.cloned.1.call-done.mine = bf16[8448,128]{1,0:T(8,128)(2,1)} async-done(((bf16[1056,128]{1,0:T(8,128)(2,1)}), bf16[8448,128]{1,0:T(8,128)(2,1)}) %all-gather.2.cloned.1.call-update) | async-done | bytes 2162704 | tf_op jit(solution)/shard_map/all_gather | solution.py:285
  86.6 1.9 %collective-permute-start = (bf16[8448,128]{1,0:T(8,128)(2,1)}, bf16[8448,128]{1,0:T(8,128)(2,1)S(1)}, u32[]{:S(2)}, u32[]{:S(2)}) collective-permute-start(bf16[8448,128]{1,0:T(8,128)(2,1)} %all-gather.2.cloned.1.call-done.mine), channel_id=1, source_target_pairs={{0,32},{32,0},{64,96},{96,64},{128,160},{160,128},{192,224},{224,1... | collective-permute-start | bytes 6488072 | tf_op jit(solution)/shard_map/ppermute | solution.py:288
  88.5 0.0 all-to-all-done.packed
  88.5 0.0 copy-start.1
  88.6 0.7 copy-done.1
  89.3 2.0 %project.1 = bf16[32,32,128]{2,1,0:T(8,128)(2,1)} custom-call(bf16[32,40,128]{2,1,0:T(8,128)(2,1)} %copy-done.1), custom_call_target="tpu_custom_call" | custom-call | tf_op jit(solution)/shard_map/project/pallas_call | solution.py:113
  91.3 12.6 %all-to-all-start.1 = ((bf16[32,32,128]{2,1,0:T(8,128)(2,1)}), bf16[32,32,128]{2,1,0:T(8,128)(2,1)S(1)}, u32[]{:S(2)}, u32[]{:S(2)}) async-start(bf16[32,32,128]{2,1,0:T(8,128)(2,1)} %project.1), calls=%async_computation.1 | async-start | bytes 524288 | tf_op jit(solution)/shard_map/all_to_all | solution.py:289
  103.9 22.9 %all-to-all-done.1 = bf16[32,32,128]{2,1,0:T(8,128)(2,1)S(1)} async-done(((bf16[32,32,128]{2,1,0:T(8,128)(2,1)}), bf16[32,32,128]{2,1,0:T(8,128)(2,1)S(1)}, u32[]{:S(2)}, u32[]{:S(2)}) %all-to-all-start.1) | async-done | bytes 262176 | tf_op jit(solution)/shard_map/all_to_all | solution.py:289
  126.8 0.0 copy-start.2
  126.8 0.0 collective-permute-done.theirs
  126.8 0.0 copy-start
  126.8 0.7 copy-done.2
  127.5 0.7 copy-done
  128.2 12.4 %score.1 = f32[32,128]{1,0:T(8,128)} custom-call(s32[1]{0:T(128)} %bitcast.group, bf16[1024,128]{1,0:T(8,128)(2,1)} %bitcast.11, bf16[8448,128]{1,0:T(8,128)(2,1)} %all-gather.2.cloned.1.call-done.mine, bf16[8448,128]{1,0:T(8,128)(2,1)} %copy-done), custom_call_target="tpu_custom_call" | custom-call | tf_op jit(solution)/shard_map/score/pallas_call | solution.py:173
  140.6 17.7 %all_to_all.15 = f32[32,1,128]{2,1,0:T(1,128)} all-to-all(f32[32,1,128]{2,1,0:T(1,128)} %bitcast.13), channel_id=1, replica_groups=mesh['blk'=16,'shard'=32] {'shard'}, dimensions={0} | all-to-all | bytes 32768 | tf_op jit(solution)/shard_map/all_to_all | solution.py:291
  158.3 2.0 %select.1 = f32[1,128]{1,0:T(1,128)} custom-call(f32[32,128]{1,0:T(8,128)} %bitcast.14), custom_call_target="tpu_custom_call" | custom-call | tf_op jit(solution)/shard_map/select/pallas_call | solution.py:269
Async XLA Ops:
  6.5 80.1 %all-gather.2.cloned.1.call-start = ((), (), s32[]{:S(2)}) async-start(), calls=%async_computation.3 | async-start | bytes 2433024 | tf_op jit(solution)/shard_map/all_gather | solution.py:285
  10.0 78.6 %all-to-all-start = ((bf16[32,40,128]{2,1,0:T(8,128)(2,1)}), bf16[32,40,128]{2,1,0:T(8,128)(2,1)S(1)}, u32[]{:S(2)}, u32[]{:S(2)}) async-start(bf16[32,40,128]{2,1,0:T(8,128)(2,1)} %pack.1), calls=%async_computation | async-start | bytes 655360 | tf_op jit(solution)/shard_map/all_to_all | solution.py:286
  86.6 40.2 %collective-permute-start = (bf16[8448,128]{1,0:T(8,128)(2,1)}, bf16[8448,128]{1,0:T(8,128)(2,1)S(1)}, u32[]{:S(2)}, u32[]{:S(2)}) collective-permute-start(bf16[8448,128]{1,0:T(8,128)(2,1)} %all-gather.2.cloned.1.call-done.mine), channel_id=1, source_target_pairs={{0,32},{32,0},{64,96},{96,64},{128,160},{160,128},{192,224},{224,1... | collective-permute-start | bytes 6488072 | tf_op jit(solution)/shard_map/ppermute | solution.py:288
  88.5 0.7 copy-start.1
  91.3 35.5 %all-to-all-start.1 = ((bf16[32,32,128]{2,1,0:T(8,128)(2,1)}), bf16[32,32,128]{2,1,0:T(8,128)(2,1)S(1)}, u32[]{:S(2)}, u32[]{:S(2)}) async-start(bf16[32,32,128]{2,1,0:T(8,128)(2,1)} %project.1), calls=%async_computation.1 | async-start | bytes 524288 | tf_op jit(solution)/shard_map/all_to_all | solution.py:289
  126.8 0.7 copy-start.2
  126.8 1.4 copy-start
Sparse Core Ops, SparseCore 0:
  10.5 76.0 all-gather.1

commit v2 on v1

--- a/solution.py
+++ b/solution.py
@@ -21,6 +21,7 @@
 MASK_ROWS = P_DEV * QUERIES // 128
 ROWS = STOCK_ROWS + MASK_ROWS
 HALF = GROUPS // 2
+STEPS = GROUPS // 4
 FOLD = 128 // QT
 FOLD_ROWS = HID_DEV // FOLD
 
@@ -56,6 +57,9 @@
         out_shape=jax.ShapeDtypeStruct((ROWS, DIM), jnp.bfloat16),
         in_specs=[vmem()] * 4,
         out_specs=vmem(),
+        cost_estimate=pl.CostEstimate(
+            flops=10**9, bytes_accessed=2 * ROWS * DIM * 2, transcendentals=0
+        ),
         name="stock",
     )(passages, cands, counts, permitted)
 
@@ -115,6 +119,9 @@
         out_shape=jax.ShapeDtypeStruct((LANES, QT, DIM), jnp.bfloat16),
         in_specs=[vmem()],
         out_specs=vmem(),
+        cost_estimate=pl.CostEstimate(
+            flops=20 * 10**9, bytes_accessed=LANES * QT * DIM * 2, transcendentals=0
+        ),
         name="project",
     )(packed)
 
@@ -149,11 +156,11 @@
             picked = jnp.where(quarter == b, mask[P_DEV * b : P_DEV * (b + 1)], picked)
         masks[side, step] = picked
 
-    @pl.when(step == HALF - 1)
+    @pl.when(step == STEPS - 1)
     def _():
-        tops = best[...].reshape(GROUPS * P_DEV, TOK)
+        tops = best[...].reshape(HALF * P_DEV, TOK)
         member = (row_index((QT, TOK)) == lane_index((QT, TOK)) // QT).astype(jnp.bfloat16)
-        scores = jnp.zeros((QT, 128), jnp.float32)
+        scores = jnp.zeros((QT, HALF * P_DEV), jnp.float32)
         for part in three_parts(tops):
             scores = scores + lax.dot_general(
                 member, part, (((1,), (1,)), ((), ())), preferred_element_type=jnp.float32
@@ -162,7 +169,7 @@
         chosen = (lane_index((QT, 128)) == wanted).astype(jnp.bfloat16)
         live = lax.dot_general(
             chosen,
-            masks[...].reshape(128, 128).astype(jnp.bfloat16),
+            masks[...].reshape(HALF * P_DEV, 128).astype(jnp.bfloat16),
             (((1,), (1,)), ((), ())),
             preferred_element_type=jnp.float32,
         )
@@ -172,20 +179,23 @@
 def score(group, queries, mine, theirs):
     return pl.pallas_call(
         score_kernel,
-        out_shape=jax.ShapeDtypeStruct((QT, 128), jnp.float32),
-        grid=(HALF,),
+        out_shape=jax.ShapeDtypeStruct((QT, HALF * P_DEV), jnp.float32),
+        grid=(STEPS,),
         in_specs=[
             pl.BlockSpec(memory_space=pltpu.SMEM),
             pl.BlockSpec((TOK, DIM), lambda i: (0, 0)),
             pl.BlockSpec((ROWS, DIM), lambda i: (i, 0)),
             pl.BlockSpec((ROWS, DIM), lambda i: (i, 0)),
         ],
-        out_specs=pl.BlockSpec((QT, 128), lambda i: (0, 0)),
+        out_specs=pl.BlockSpec((QT, HALF * P_DEV), lambda i: (0, 0)),
         scratch_shapes=[
             pltpu.VMEM((DIM, TOK), jnp.bfloat16),
-            pltpu.VMEM((2, HALF, P_DEV, TOK), jnp.float32),
-            pltpu.VMEM((2, HALF, P_DEV, 128), jnp.float32),
+            pltpu.VMEM((2, STEPS, P_DEV, TOK), jnp.float32),
+            pltpu.VMEM((2, STEPS, P_DEV, 128), jnp.float32),
         ],
+        cost_estimate=pl.CostEstimate(
+            flops=40 * 10**9, bytes_accessed=2 * STEPS * ROWS * DIM * 2, transcendentals=0
+        ),
         name="score",
     )(group, queries, mine, theirs)
 
@@ -275,19 +285,30 @@
     )(table)
 
 
+def turned(steps):
+    return [(i, (i + steps) % GROUPS) for i in range(GROUPS)]
+
+
 def body(hidden, proj_weight, passages, cands, counts, permitted):
     group = lax.axis_index("blk").astype(jnp.int32).reshape(1)
     slots = cands.reshape(QUERIES, CAND).T
+    packed = pack(hidden, proj_weight)
+    passages, packed = lax.optimization_barrier((passages, packed))
     own = stock(
         passages.reshape(STOCK_ROWS, DIM), slots, counts.reshape(1, QUERIES), permitted
     )
-    same_core = [list(range(core, GROUPS, 2)) for core in range(2)]
-    mine = lax.all_gather(own, "blk", axis=0, tiled=True, axis_index_groups=same_core)
-    packed = lax.all_to_all(pack(hidden, proj_weight), "shard", 0, 0, tiled=True)
-    rows = project(packed)
-    theirs = lax.ppermute(mine, "blk", [(i, i ^ 1) for i in range(GROUPS)])
+    along_x = [lax.ppermute(own, "blk", turned(4 * x)) for x in (1, 3, 2)]
+    near = jnp.concatenate([own, *along_x])
+    far = lax.ppermute(near, "blk", [(i, i ^ 2) for i in range(GROUPS)])
+    other_core = [(i, i ^ 1) for i in range(GROUPS)]
+    rows = project(lax.all_to_all(packed, "shard", 0, 0, tiled=True))
+    held, rows = lax.optimization_barrier((near, rows))
+    near_other = lax.ppermute(held, "blk", other_core)
+    far_other = lax.ppermute(far, "blk", other_core)
     queries = lax.all_to_all(rows, "shard", 0, 0, tiled=True).reshape(TOK, DIM)
-    table = score(group, queries, mine, theirs)
+    first = score(group, queries, near, near_other)
+    second = score(group, queries, far, far_other)
+    table = jnp.concatenate([first, second], axis=1)
     entries = lax.all_to_all(table.reshape(LANES, 1, 128), "shard", 0, 0, tiled=True)
     return select(entries.reshape(LANES, 128))
 

time: 168 us -> 119 us (0.71)
  the two profiles are of different devices: /device:TPU:2 before, /device:TPU:8 now
where the time goes in v2:
time: 119 us; the launch traced here: 118 us
  starting transfers between devices  48.6 us (41%)
  waiting for transfers between devices  27.2 us (23%)
  Pallas kernels  21.9 us (18%)
  blocking collectives  16.8 us (14%)
  other arithmetic  1.81 us (2%)
  local copies, waits for them, and re-layouts  1.46 us (1%)
    all_to_all x1, blocking collectives, body(): lax.all_to_all(table.reshape(LANES, 1, 128), 'shard', 0, 0, tiled=True)  16.8 us
    all_to_all x1, starting transfers between devices, body(): rows = project(lax.all_to_all(packed, 'shard', 0, 0, tiled=True))  16.7 us
    pallas_call x2, Pallas kernels, score(): pl.pallas_call(score_kernel, out_shape=jax.ShapeDtypeStruct((QT, HALF * P...  14.4 us
    all_to_all x1, waiting for transfers between devices, body(): queries = lax.all_to_all(rows, 'shard', 0, 0, tiled=True).reshape(TOK, DIM)  14.3 us
    all_to_all x1, starting transfers between devices, body(): queries = lax.all_to_all(rows, 'shard', 0, 0, tiled=True).reshape(TOK, DIM)  13.1 us
    ppermute x3, starting transfers between devices, body(): along_x = [lax.ppermute(own, 'blk', turned(4 * x)) for x in (1, 3, 2)]  10.8 us
    ppermute x3, waiting for transfers between devices, body(): along_x = [lax.ppermute(own, 'blk', turned(4 * x)) for x in (1, 3, 2)]  7.61 us
    ppermute x1, waiting for transfers between devices, body(): far = lax.ppermute(near, 'blk', [(i, i ^ 2) for i in range(GROUPS)])  5.28 us
  transfers between devices with their start and end apart: 8, of which 5 were waited for; matrix products, arithmetic and copies ran while one was open for 1% of the time, Pallas kernels for 9%

profile of v2, /device:TPU:8, one launch (start us, length us, event | category | flops | bytes accessed | tf_op | source)
XLA Modules:
  0.0 117.9 jit_solution(18227366090543365304)
XLA Ops:
  0.0 1.7 %pack.1 = bf16[32,40,128]{2,1,0:T(8,128)(2,1)} custom-call(bf16[32,1024]{1,0:T(8,128)(2,1)} %hidden.1, bf16[32,128]{1,0:T(8,128)(2,1)} %weight.1), custom_call_target="tpu_custom_call" | custom-call | tf_op jit(solution)/shard_map/pack/pallas_call | solution.py:84
  1.7 16.7 %all-to-all-start = ((bf16[32,40,128]{2,1,0:T(8,128)(2,1)}), bf16[32,40,128]{2,1,0:T(8,128)(2,1)S(1)}, u32[]{:S(2)}, u32[]{:S(2)}) async-start(bf16[32,40,128]{2,1,0:T(8,128)(2,1)} %pack.1), calls=%async_computation | async-start | bytes 655360 | tf_op jit(solution)/shard_map/all_to_all | solution.py:304
  18.4 1.7 %stock.1 = bf16[1056,128]{1,0:T(8,128)(2,1)} custom-call(bf16[1024,128]{1,0:T(8,128)(2,1)} %bitcast.15, s32[4,512]{1,0:T(4,128)} %bitcast.16, s32[1,512]{1,0:T(1,128)} %bitcast.17, s32[1,512]{1,0:T(1,128)} %permitted.1), custom_call_target="tpu_custom_call" | custom-call | flops 1000000000 | bytes 540672 | tf_op jit(solution)/shard_map/stock/pallas_call | solution.py:55
  20.1 4.9 %collective-permute-start.2 = (bf16[1056,128]{1,0:T(8,128)(2,1)}, bf16[1056,128]{1,0:T(8,128)(2,1)S(1)}, u32[]{:S(2)}, u32[]{:S(2)}) collective-permute-start(bf16[1056,128]{1,0:T(8,128)(2,1)} %stock.1), channel_id=1, source_target_pairs={{0,256},{32,288},{64,320},{96,352},{128,384},{160,416},{192,448},{... | collective-permute-start | bytes 811016 | tf_op jit(solution)/shard_map/ppermute | solution.py:300
  25.1 3.0 %collective-permute-start.1 = (bf16[1056,128]{1,0:T(8,128)(2,1)}, bf16[1056,128]{1,0:T(8,128)(2,1)S(1)}, u32[]{:S(2)}, u32[]{:S(2)}) collective-permute-start(bf16[1056,128]{1,0:T(8,128)(2,1)} %stock.1), channel_id=1, source_target_pairs={{0,384},{32,416},{64,448},{96,480},{128,0},{160,32},{192,64},{224,... | collective-permute-start | bytes 811016 | tf_op jit(solution)/shard_map/ppermute | solution.py:300
  28.1 2.8 %collective-permute-start = (bf16[1056,128]{1,0:T(8,128)(2,1)}, bf16[1056,128]{1,0:T(8,128)(2,1)S(1)}, u32[]{:S(2)}, u32[]{:S(2)}) collective-permute-start(bf16[1056,128]{1,0:T(8,128)(2,1)} %stock.1), channel_id=1, source_target_pairs={{0,128},{32,160},{64,192},{96,224},{128,256},{160,288},{192,320},{... | collective-permute-start | bytes 811016 | tf_op jit(solution)/shard_map/ppermute | solution.py:300
  30.9 0.5 collective-permute-done.2
  31.4 5.9 %collective-permute-done.1 = bf16[1056,128]{1,0:T(8,128)(2,1)S(1)} collective-permute-done((bf16[1056,128]{1,0:T(8,128)(2,1)}, bf16[1056,128]{1,0:T(8,128)(2,1)S(1)}, u32[]{:S(2)}, u32[]{:S(2)}) %collective-permute-start.1) | collective-permute-done | bytes 270368 | tf_op jit(solution)/shard_map/ppermute | solution.py:300
  37.3 1.3 %collective-permute-done = bf16[1056,128]{1,0:T(8,128)(2,1)S(1)} collective-permute-done((bf16[1056,128]{1,0:T(8,128)(2,1)}, bf16[1056,128]{1,0:T(8,128)(2,1)S(1)}, u32[]{:S(2)}, u32[]{:S(2)}) %collective-permute-start) | collective-permute-done | bytes 270368 | tf_op jit(solution)/shard_map/ppermute | solution.py:300
  38.5 1.0 pad_maximum_fusion.mine
  39.6 0.0 copy-start
  39.6 4.2 %collective-permute-start.4 = (bf16[4224,128]{1,0:T(8,128)(2,1)S(1)}, bf16[4224,128]{1,0:T(8,128)(2,1)S(1)}, u32[]{:S(2)}, u32[]{:S(2)}) collective-permute-start(bf16[4224,128]{1,0:T(8,128)(2,1)S(1)} %pad_maximum_fusion.mine), channel_id=1, source_target_pairs={{0,64},{32,96},{64,0},{96,32},{128,192},{160,224},{192,128},{224,1... | collective-permute-start | bytes 3244040 | tf_op jit(solution)/shard_map/ppermute | solution.py:302
  43.8 0.0 all-to-all-done.packed
  43.8 0.0 copy-start.1
  43.8 0.7 copy-done.1
  44.5 2.0 %project.1 = bf16[32,32,128]{2,1,0:T(8,128)(2,1)} custom-call(bf16[32,40,128]{2,1,0:T(8,128)(2,1)} %copy-done.1), custom_call_target="tpu_custom_call" | custom-call | flops 20000000000 | bytes 262144 | tf_op jit(solution)/shard_map/project/pallas_call | solution.py:117
  46.6 0.0 copy-done
  46.6 1.9 %collective-permute-start.3 = (bf16[4224,128]{1,0:T(8,128)(2,1)S(1)}, bf16[4224,128]{1,0:T(8,128)(2,1)}, u32[]{:S(2)}, u32[]{:S(2)}) collective-permute-start(bf16[4224,128]{1,0:T(8,128)(2,1)S(1)} %pad_maximum_fusion.mine), channel_id=1, source_target_pairs={{0,32},{32,0},{64,96},{96,64},{128,160},{160,128},{192,224},{224,1... | collective-permute-start | bytes 3244040 | tf_op jit(solution)/shard_map/ppermute | solution.py:306
  48.5 13.1 %all-to-all-start.1 = ((bf16[32,32,128]{2,1,0:T(8,128)(2,1)}), bf16[32,32,128]{2,1,0:T(8,128)(2,1)S(1)}, u32[]{:S(2)}, u32[]{:S(2)}) async-start(bf16[32,32,128]{2,1,0:T(8,128)(2,1)} %project.1), calls=%async_computation.1 | async-start | bytes 524288 | tf_op jit(solution)/shard_map/all_to_all | solution.py:308
  61.6 5.3 %collective-permute-done.4.mine = bf16[4224,128]{1,0:T(8,128)(2,1)S(1)} collective-permute-done((bf16[4224,128]{1,0:T(8,128)(2,1)S(1)}, bf16[4224,128]{1,0:T(8,128)(2,1)S(1)}, u32[]{:S(2)}, u32[]{:S(2)}) %collective-permute-start.4) | collective-permute-done | bytes 1081376 | tf_op jit(solution)/shard_map/ppermute | solution.py:302
  66.9 1.9 %collective-permute-start.5 = (bf16[4224,128]{1,0:T(8,128)(2,1)S(1)}, bf16[4224,128]{1,0:T(8,128)(2,1)}, u32[]{:S(2)}, u32[]{:S(2)}) collective-permute-start(bf16[4224,128]{1,0:T(8,128)(2,1)S(1)} %collective-permute-done.4.mine), channel_id=1, source_target_pairs={{0,32},{32,0},{64,96},{96,64},{128,160},{160,128},{192,224},{224,1... | collective-permute-start | bytes 3244040 | tf_op jit(solution)/shard_map/ppermute | solution.py:307
  68.8 14.3 %all-to-all-done.1 = bf16[32,32,128]{2,1,0:T(8,128)(2,1)S(1)} async-done(((bf16[32,32,128]{2,1,0:T(8,128)(2,1)}), bf16[32,32,128]{2,1,0:T(8,128)(2,1)S(1)}, u32[]{:S(2)}, u32[]{:S(2)}) %all-to-all-start.1) | async-done | bytes 262176 | tf_op jit(solution)/shard_map/all_to_all | solution.py:308
  83.2 0.0 collective-permute-done.3.theirs
  83.2 0.7 copy-done.2
  83.9 7.2 %score.2 = f32[32,64]{1,0:T(8,128)} custom-call(s32[1]{0:T(128)} %bitcast.group, bf16[1024,128]{1,0:T(8,128)(2,1)} %bitcast.11, bf16[4224,128]{1,0:T(8,128)(2,1)} %copy-done, bf16[4224,128]{1,0:T(8,128)(2,1)} %collective-permute-done.3.theirs), custom_call_target="tpu_custom_call" | custom-call | flops 40000000000 | bytes 2162688 | tf_op jit(solution)/shard_map/score/pallas_call | solution.py:180
  91.1 0.0 copy-done.4
  91.1 0.0 collective-permute-done.5.theirs
  91.1 7.2 %score.3 = f32[32,64]{1,0:T(8,128)} custom-call(s32[1]{0:T(128)} %bitcast.group, bf16[1024,128]{1,0:T(8,128)(2,1)} %bitcast.12, bf16[4224,128]{1,0:T(8,128)(2,1)} %copy-done.4, bf16[4224,128]{1,0:T(8,128)(2,1)} %collective-permute-done.5.theirs), custom_call_target="tpu_custom_call" | custom-call | flops 40000000000 | bytes 2162688 | tf_op jit(solution)/shard_map/score/pallas_call | solution.py:180
  98.3 0.0 copy-done.3
  98.3 0.8 pad_maximum_fusion.1
  99.1 16.8 %all_to_all.15 = f32[32,1,128]{2,1,0:T(1,128)} all-to-all(f32[32,1,128]{2,1,0:T(1,128)S(1)} %bitcast.13), channel_id=1, replica_groups=mesh['blk'=16,'shard'=32] {'shard'}, dimensions={0} | all-to-all | bytes 32768 | tf_op jit(solution)/shard_map/all_to_all | solution.py:312
  115.9 2.0 %select.1 = f32[1,128]{1,0:T(1,128)} custom-call(f32[32,128]{1,0:T(8,128)} %bitcast.14), custom_call_target="tpu_custom_call" | custom-call | tf_op jit(solution)/shard_map/select/pallas_call | solution.py:279
  (3 shorter events, 0.0 us)
Async XLA Ops:
  1.7 42.1 %all-to-all-start = ((bf16[32,40,128]{2,1,0:T(8,128)(2,1)}), bf16[32,40,128]{2,1,0:T(8,128)(2,1)S(1)}, u32[]{:S(2)}, u32[]{:S(2)}) async-start(bf16[32,40,128]{2,1,0:T(8,128)(2,1)} %pack.1), calls=%async_computation | async-start | bytes 655360 | tf_op jit(solution)/shard_map/all_to_all | solution.py:304
  20.1 11.3 %collective-permute-start.2 = (bf16[1056,128]{1,0:T(8,128)(2,1)}, bf16[1056,128]{1,0:T(8,128)(2,1)S(1)}, u32[]{:S(2)}, u32[]{:S(2)}) collective-permute-start(bf16[1056,128]{1,0:T(8,128)(2,1)} %stock.1), channel_id=1, source_target_pairs={{0,256},{32,288},{64,320},{96,352},{128,384},{160,416},{192,448},{... | collective-permute-start | bytes 811016 | tf_op jit(solution)/shard_map/ppermute | solution.py:300
  25.1 12.2 %collective-permute-start.1 = (bf16[1056,128]{1,0:T(8,128)(2,1)}, bf16[1056,128]{1,0:T(8,128)(2,1)S(1)}, u32[]{:S(2)}, u32[]{:S(2)}) collective-permute-start(bf16[1056,128]{1,0:T(8,128)(2,1)} %stock.1), channel_id=1, source_target_pairs={{0,384},{32,416},{64,448},{96,480},{128,0},{160,32},{192,64},{224,... | collective-permute-start | bytes 811016 | tf_op jit(solution)/shard_map/ppermute | solution.py:300
  28.1 10.4 %collective-permute-start = (bf16[1056,128]{1,0:T(8,128)(2,1)}, bf16[1056,128]{1,0:T(8,128)(2,1)S(1)}, u32[]{:S(2)}, u32[]{:S(2)}) collective-permute-start(bf16[1056,128]{1,0:T(8,128)(2,1)} %stock.1), channel_id=1, source_target_pairs={{0,128},{32,160},{64,192},{96,224},{128,256},{160,288},{192,320},{... | collective-permute-start | bytes 811016 | tf_op jit(solution)/shard_map/ppermute | solution.py:300
  39.6 7.0 %copy-start = (bf16[4224,128]{1,0:T(8,128)(2,1)}, bf16[4224,128]{1,0:T(8,128)(2,1)S(1)}, u32[]{:S(2)}) copy-start(bf16[4224,128]{1,0:T(8,128)(2,1)S(1)} %pad_maximum_fusion.mine) | copy-start | bytes 3244036
  39.6 27.3 %collective-permute-start.4 = (bf16[4224,128]{1,0:T(8,128)(2,1)S(1)}, bf16[4224,128]{1,0:T(8,128)(2,1)S(1)}, u32[]{:S(2)}, u32[]{:S(2)}) collective-permute-start(bf16[4224,128]{1,0:T(8,128)(2,1)S(1)} %pad_maximum_fusion.mine), channel_id=1, source_target_pairs={{0,64},{32,96},{64,0},{96,32},{128,192},{160,224},{192,128},{224,1... | collective-permute-start | bytes 3244040 | tf_op jit(solution)/shard_map/ppermute | solution.py:302
  43.8 0.7 copy-start.1
  46.6 36.6 %collective-permute-start.3 = (bf16[4224,128]{1,0:T(8,128)(2,1)S(1)}, bf16[4224,128]{1,0:T(8,128)(2,1)}, u32[]{:S(2)}, u32[]{:S(2)}) collective-permute-start(bf16[4224,128]{1,0:T(8,128)(2,1)S(1)} %pad_maximum_fusion.mine), channel_id=1, source_target_pairs={{0,32},{32,0},{64,96},{96,64},{128,160},{160,128},{192,224},{224,1... | collective-permute-start | bytes 3244040 | tf_op jit(solution)/shard_map/ppermute | solution.py:306
  48.5 34.7 %all-to-all-start.1 = ((bf16[32,32,128]{2,1,0:T(8,128)(2,1)}), bf16[32,32,128]{2,1,0:T(8,128)(2,1)S(1)}, u32[]{:S(2)}, u32[]{:S(2)}) async-start(bf16[32,32,128]{2,1,0:T(8,128)(2,1)} %project.1), calls=%async_computation.1 | async-start | bytes 524288 | tf_op jit(solution)/shard_map/all_to_all | solution.py:308
  66.9 24.1 %copy-start.4 = (bf16[4224,128]{1,0:T(8,128)(2,1)}, bf16[4224,128]{1,0:T(8,128)(2,1)S(1)}, u32[]{:S(2)}) copy-start(bf16[4224,128]{1,0:T(8,128)(2,1)S(1)} %collective-permute-done.4.mine) | copy-start | bytes 3244036
  66.9 24.1 %collective-permute-start.5 = (bf16[4224,128]{1,0:T(8,128)(2,1)S(1)}, bf16[4224,128]{1,0:T(8,128)(2,1)}, u32[]{:S(2)}, u32[]{:S(2)}) collective-permute-start(bf16[4224,128]{1,0:T(8,128)(2,1)S(1)} %collective-permute-done.4.mine), channel_id=1, source_target_pairs={{0,32},{32,0},{64,96},{96,64},{128,160},{160,128},{192,224},{224,1... | collective-permute-start | bytes 3244040 | tf_op jit(solution)/shard_map/ppermute | solution.py:307
  83.2 0.7 copy-start.2
  91.1 7.2 %copy-start.3 = (f32[32,64]{1,0:T(8,128)S(1)}, f32[32,64]{1,0:T(8,128)}, u32[]{:S(2)}) copy-start(f32[32,64]{1,0:T(8,128)} %score.2) | copy-start | bytes 24580

commit v3 on v1

--- a/solution.py
+++ b/solution.py
@@ -20,13 +20,17 @@
 STOCK_ROWS = P_DEV * PT
 MASK_ROWS = P_DEV * QUERIES // 128
 ROWS = STOCK_ROWS + MASK_ROWS
-HALF = GROUPS // 2
+STEPS = GROUPS // 4
 FOLD = 128 // QT
 FOLD_ROWS = HID_DEV // FOLD
 
 
 def vmem():
     return pl.BlockSpec(memory_space=pltpu.VMEM)
+
+
+def limit(mebibytes):
+    return pltpu.CompilerParams(vmem_limit_bytes=mebibytes * 2**20)
 
 
 def lane_index(shape):
@@ -48,16 +52,6 @@
         live = jnp.where(use == slots, 1.0, live)
     parts = [live[:, 128 * b : 128 * (b + 1)] for b in range(QUERIES // 128)]
     out[STOCK_ROWS:ROWS, :] = jnp.concatenate(parts, axis=0).astype(jnp.bfloat16)
-
-
-def stock(passages, cands, counts, permitted):
-    return pl.pallas_call(
-        stock_kernel,
-        out_shape=jax.ShapeDtypeStruct((ROWS, DIM), jnp.bfloat16),
-        in_specs=[vmem()] * 4,
-        out_specs=vmem(),
-        name="stock",
-    )(passages, cands, counts, permitted)
 
 
 def pack_kernel(hidden, weight, out):
@@ -76,14 +70,61 @@
             out[tile * FOLD + k] = both.astype(jnp.bfloat16)
 
 
-def pack(hidden, weight):
-    return pl.pallas_call(
-        pack_kernel,
-        out_shape=jax.ShapeDtypeStruct((LANES, FOLD_ROWS + HID_DEV, 128), jnp.bfloat16),
+def prepare_kernel(hidden, weight, passages, cands, counts, permitted, packed, own):
+    pack_kernel(hidden, weight, packed)
+    stock_kernel(passages, cands, counts, permitted, own)
+
+
+def prepare(hidden, weight, passages, cands, counts, permitted):
+    return pl.pallas_call(
+        prepare_kernel,
+        out_shape=(
+            jax.ShapeDtypeStruct((LANES, FOLD_ROWS + HID_DEV, 128), jnp.bfloat16),
+            jax.ShapeDtypeStruct((ROWS, DIM), jnp.bfloat16),
+        ),
+        in_specs=[vmem()] * 6,
+        out_specs=(vmem(), vmem()),
+        compiler_params=limit(56),
+        name="prepare",
+    )(hidden, weight, passages, cands, counts, permitted)
+
+
+def both_kernel(own, across, out):
+    out[0:ROWS, :] = own[...]
+    out[ROWS : 2 * ROWS, :] = across[...]
+
+
+def both(own, across):
+    return pl.pallas_call(
+        both_kernel,
+        out_shape=jax.ShapeDtypeStruct((2 * ROWS, DIM), jnp.bfloat16),
         in_specs=[vmem()] * 2,
         out_specs=vmem(),
-        name="pack",
-    )(hidden, weight)
+        cost_estimate=pl.CostEstimate(
+            flops=40 * 10**9, bytes_accessed=4 * ROWS * DIM * 2, transcendentals=0
+        ),
+        compiler_params=limit(8),
+        name="both",
+    )(own, across)
+
+
+def all_four_kernel(*refs):
+    for i, ref in enumerate(refs[:4]):
+        refs[4][2 * ROWS * i : 2 * ROWS * (i + 1), :] = ref[...]
+
+
+def all_four(*pairs):
+    return pl.pallas_call(
+        all_four_kernel,
+        out_shape=jax.ShapeDtypeStruct((8 * ROWS, DIM), jnp.bfloat16),
+        in_specs=[vmem()] * 4,
+        out_specs=vmem(),
+        cost_estimate=pl.CostEstimate(
+            flops=10 * 10**9, bytes_accessed=16 * ROWS * DIM * 2, transcendentals=0
+        ),
+        compiler_params=limit(14),
+        name="all_four",
+    )(*pairs)
 
 
 def project_kernel(packed, out):
@@ -115,6 +156,10 @@
         out_shape=jax.ShapeDtypeStruct((LANES, QT, DIM), jnp.bfloat16),
         in_specs=[vmem()],
         out_specs=vmem(),
+        cost_estimate=pl.CostEstimate(
+            flops=20 * 10**9, bytes_accessed=LANES * QT * DIM * 2, transcendentals=0
+        ),
+        compiler_params=limit(8),
         name="project",
     )(packed)
 
@@ -127,15 +172,30 @@
     return first, second, third
 
 
-def score_kernel(group, queries, mine, theirs, out, turned, best, masks):
+def turn_kernel(queries, out):
+    out[...] = queries[...].astype(jnp.float32).T.astype(jnp.bfloat16)
+
+
+def turn(queries):
+    return pl.pallas_call(
+        turn_kernel,
+        out_shape=jax.ShapeDtypeStruct((DIM, TOK), jnp.bfloat16),
+        in_specs=[vmem()],
+        out_specs=vmem(),
+        cost_estimate=pl.CostEstimate(
+            flops=40 * 10**9, bytes_accessed=2 * TOK * DIM * 2, transcendentals=0
+        ),
+        compiler_params=limit(8),
+        name="turn",
+    )(queries)
+
+
+def score_kernel(group, turned, *refs):
+    blocks, (out, best, masks) = refs[:4], refs[4:]
     step = pl.program_id(0)
 
-    @pl.when(step == 0)
-    def _():
-        turned[...] = queries[...].astype(jnp.float32).T.astype(jnp.bfloat16)
-
     quarter = group[0] // FOLD
-    for side, block in enumerate((mine, theirs)):
+    for side, block in enumerate(blocks):
         for c in range(TOK // 256):
             part = turned[:, 256 * c : 256 * (c + 1)]
             similarity = jnp.dot(
@@ -149,11 +209,11 @@
             picked = jnp.where(quarter == b, mask[P_DEV * b : P_DEV * (b + 1)], picked)
         masks[side, step] = picked
 
-    @pl.when(step == HALF - 1)
+    @pl.when(step == STEPS - 1)
     def _():
         tops = best[...].reshape(GROUPS * P_DEV, TOK)
         member = (row_index((QT, TOK)) == lane_index((QT, TOK)) // QT).astype(jnp.bfloat16)
-        scores = jnp.zeros((QT, 128), jnp.float32)
+        scores = jnp.zeros((QT, GROUPS * P_DEV), jnp.float32)
         for part in three_parts(tops):
             scores = scores + lax.dot_general(
                 member, part, (((1,), (1,)), ((), ())), preferred_element_type=jnp.float32
@@ -162,7 +222,7 @@
         chosen = (lane_index((QT, 128)) == wanted).astype(jnp.bfloat16)
         live = lax.dot_general(
             chosen,
-            masks[...].reshape(128, 128).astype(jnp.bfloat16),
+            masks[...].reshape(GROUPS * P_DEV, 128).astype(jnp.bfloat16),
             (((1,), (1,)), ((), ())),
             preferred_element_type=jnp.float32,
         )
@@ -172,22 +232,24 @@
 def score(group, queries, mine, theirs):
     return pl.pallas_call(
         score_kernel,
-        out_shape=jax.ShapeDtypeStruct((QT, 128), jnp.float32),
-        grid=(HALF,),
+        out_shape=jax.ShapeDtypeStruct((QT, GROUPS * P_DEV), jnp.float32),
+        grid=(STEPS,),
         in_specs=[
             pl.BlockSpec(memory_space=pltpu.SMEM),
-            pl.BlockSpec((TOK, DIM), lambda i: (0, 0)),
-            pl.BlockSpec((ROWS, DIM), lambda i: (i, 0)),
-            pl.BlockSpec((ROWS, DIM), lambda i: (i, 0)),
+            pl.BlockSpec((DIM, TOK), lambda i: (0, 0)),
+            *[pl.BlockSpec((ROWS, DIM), lambda i, at=at: (i + at, 0)) for at in (0, STEPS)] * 2,
         ],
-        out_specs=pl.BlockSpec((QT, 128), lambda i: (0, 0)),
+        out_specs=pl.BlockSpec((QT, GROUPS * P_DEV), lambda i: (0, 0)),
         scratch_shapes=[
-            pltpu.VMEM((DIM, TOK), jnp.bfloat16),
-            pltpu.VMEM((2, HALF, P_DEV, TOK), jnp.float32),
-            pltpu.VMEM((2, HALF, P_DEV, 128), jnp.float32),
+            pltpu.VMEM((4, STEPS, P_DEV, TOK), jnp.float32),
+            pltpu.VMEM((4, STEPS, P_DEV, 128), jnp.float32),
         ],
+        cost_estimate=pl.CostEstimate(
+            flops=40 * 10**9, bytes_accessed=GROUPS * ROWS * DIM * 2, transcendentals=0
+        ),
+        compiler_params=limit(16),
         name="score",
-    )(group, queries, mine, theirs)
+    )(group, queries, mine, mine, theirs, theirs)
 
 
 def split_exchange(arrays, distance):
@@ -271,23 +333,34 @@
         out_shape=jax.ShapeDtypeStruct((1, K), jnp.float32),
         in_specs=[vmem()],
         out_specs=vmem(),
+        compiler_params=limit(8),
         name="select",
     )(table)
+
+
+def turned(steps):
+    return [(i, (i + steps) % GROUPS) for i in range(GROUPS)]
 
 
 def body(hidden, proj_weight, passages, cands, counts, permitted):
     group = lax.axis_index("blk").astype(jnp.int32).reshape(1)
     slots = cands.reshape(QUERIES, CAND).T
-    own = stock(
-        passages.reshape(STOCK_ROWS, DIM), slots, counts.reshape(1, QUERIES), permitted
+    packed, own = prepare(
+        hidden,
+        proj_weight,
+        passages.reshape(STOCK_ROWS, DIM),
+        slots,
+        counts.reshape(1, QUERIES),
+        permitted,
     )
-    same_core = [list(range(core, GROUPS, 2)) for core in range(2)]
-    mine = lax.all_gather(own, "blk", axis=0, tiled=True, axis_index_groups=same_core)
-    packed = lax.all_to_all(pack(hidden, proj_weight), "shard", 0, 0, tiled=True)
-    rows = project(packed)
+    across = lax.ppermute(own, "blk", [(i, i ^ 2) for i in range(GROUPS)])
+    pair = both(own, across)
+    along_x = [lax.ppermute(pair, "blk", turned(4 * x)) for x in (1, 3, 2)]
+    rows = project(lax.all_to_all(packed, "shard", 0, 0, tiled=True))
+    mine = all_four(pair, *along_x)
     theirs = lax.ppermute(mine, "blk", [(i, i ^ 1) for i in range(GROUPS)])
     queries = lax.all_to_all(rows, "shard", 0, 0, tiled=True).reshape(TOK, DIM)
-    table = score(group, queries, mine, theirs)
+    table = score(group, turn(queries), mine, theirs)
     entries = lax.all_to_all(table.reshape(LANES, 1, 128), "shard", 0, 0, tiled=True)
     return select(entries.reshape(LANES, 128))
 

time: 168 us -> 103 us (0.61)
  the two profiles are of different devices: /device:TPU:2 before, /device:TPU:4 now
where the time goes in v3:
time: 103 us; the launch traced here: 102 us
  starting transfers between devices  34.9 us (34%)
  waiting for transfers between devices  31 us (30%)
  blocking collectives  16.3 us (16%)
  Pallas kernels  15.5 us (15%)
  local copies, waits for them, and re-layouts  4.63 us (4%)
    all_to_all x1, blocking collectives, body(): lax.all_to_all(table.reshape(LANES, 1, 128), 'shard', 0, 0, tiled=True)  16.3 us
    all_to_all x1, waiting for transfers between devices, body(): queries = lax.all_to_all(rows, 'shard', 0, 0, tiled=True).reshape(TOK, DIM)  16.2 us
    all_to_all x1, starting transfers between devices, body(): rows = project(lax.all_to_all(packed, 'shard', 0, 0, tiled=True))  15.6 us
    all_to_all x1, waiting for transfers between devices, body(): rows = project(lax.all_to_all(packed, 'shard', 0, 0, tiled=True))  14.8 us
    pallas_call x1, Pallas kernels, score(): pl.pallas_call(score_kernel, out_shape=jax.ShapeDtypeStruct((QT, GROUPS *...  10.9 us
    ppermute x3, starting transfers between devices, body(): along_x = [lax.ppermute(pair, 'blk', turned(4 * x)) for x in (1, 3, 2)]  8.4 us
    ppermute x1, starting transfers between devices, body(): across = lax.ppermute(own, 'blk', [(i, i ^ 2) for i in range(GROUPS)])  5.09 us
    unnamed x10, local copies, waits for them, and re-layouts  4.63 us
  transfers between devices with their start and end apart: 7, of which 2 were waited for; matrix products, arithmetic and copies ran while one was open for 0% of the time, Pallas kernels for 1%

profile of v3, /device:TPU:4, one launch (start us, length us, event | category | flops | bytes accessed | tf_op | source)
XLA Modules:
  0.0 102.5 jit_solution(347599321807261503)
XLA Ops:
  0.0 1.9 %prepare.1 = (bf16[32,40,128]{2,1,0:T(8,128)(2,1)}, bf16[1056,128]{1,0:T(8,128)(2,1)}) custom-call(bf16[32,1024]{1,0:T(8,128)(2,1)} %hidden.1, bf16[32,128]{1,0:T(8,128)(2,1)} %weight.1, bf16[1024,128]{1,0:T(8,128)(2,1)} %bitcast.14, s32[4,512]{1,0:T(4,128)} %bitcast.15, s32[1,512]{1,0:T(1,128)} %bitcast.16, s32[1,512]{1,0:T(1,128)} %permitted.1), custom_call_target="tpu_custom_call" | custom-call | tf_op jit(solution)/shard_map/prepare/pallas_call | solution.py:79
  1.9 5.1 %collective-permute-start = (bf16[1056,128]{1,0:T(8,128)(2,1)}, bf16[1056,128]{1,0:T(8,128)(2,1)S(1)}, u32[]{:S(2)}, u32[]{:S(2)}) collective-permute-start(bf16[1056,128]{1,0:T(8,128)(2,1)} %get-tuple-element.8.own), channel_id=1, source_target_pairs={{0,64},{32,96},{64,0},{96,32},{128,192},{160,224},{192,128},{224,1... | collective-permute-start | bytes 811016 | tf_op jit(solution)/shard_map/ppermute | solution.py:356
  7.0 15.6 %all-to-all-start = ((bf16[32,40,128]{2,1,0:T(8,128)(2,1)}), bf16[32,40,128]{2,1,0:T(8,128)(2,1)S(1)}, u32[]{:S(2)}, u32[]{:S(2)}) async-start(bf16[32,40,128]{2,1,0:T(8,128)(2,1)} %get-tuple-element.7), calls=%async_computation | async-start | bytes 655360 | tf_op jit(solution)/shard_map/all_to_all | solution.py:359
  22.6 0.0 collective-permute-done.across
  22.6 0.0 copy-start.4
  22.7 0.9 copy-done.4
  23.6 2.4 %collective-permute-start.3 = (bf16[2112,128]{1,0:T(8,128)(2,1)S(1)}, bf16[2112,128]{1,0:T(8,128)(2,1)S(1)}, u32[]{:S(2)}, u32[]{:S(2)}) collective-permute-start(bf16[2112,128]{1,0:T(8,128)(2,1)S(1)} %both.1.refs_0_), channel_id=1, source_target_pairs={{0,256},{32,288},{64,320},{96,352},{128,384},{160,416},{192,448},{... | collective-permute-start | bytes 1622024 | tf_op jit(solution)/shard_map/ppermute | solution.py:358
  26.1 4.1 %collective-permute-start.2 = (bf16[2112,128]{1,0:T(8,128)(2,1)S(1)}, bf16[2112,128]{1,0:T(8,128)(2,1)S(1)}, u32[]{:S(2)}, u32[]{:S(2)}) collective-permute-start(bf16[2112,128]{1,0:T(8,128)(2,1)S(1)} %both.1.refs_0_), channel_id=1, source_target_pairs={{0,384},{32,416},{64,448},{96,480},{128,0},{160,32},{192,64},{224,... | collective-permute-start | bytes 1622024 | tf_op jit(solution)/shard_map/ppermute | solution.py:358
  30.1 1.9 %collective-permute-start.1 = (bf16[2112,128]{1,0:T(8,128)(2,1)S(1)}, bf16[2112,128]{1,0:T(8,128)(2,1)S(1)}, u32[]{:S(2)}, u32[]{:S(2)}) collective-permute-start(bf16[2112,128]{1,0:T(8,128)(2,1)S(1)} %both.1.refs_0_), channel_id=1, source_target_pairs={{0,128},{32,160},{64,192},{96,224},{128,256},{160,288},{192,320},{... | collective-permute-start | bytes 1622024 | tf_op jit(solution)/shard_map/ppermute | solution.py:358
  32.1 14.8 %all-to-all-done.packed = bf16[32,40,128]{2,1,0:T(8,128)(2,1)S(1)} async-done(((bf16[32,40,128]{2,1,0:T(8,128)(2,1)}), bf16[32,40,128]{2,1,0:T(8,128)(2,1)S(1)}, u32[]{:S(2)}, u32[]{:S(2)}) %all-to-all-start) | async-done | bytes 327712 | tf_op jit(solution)/shard_map/all_to_all | solution.py:359
  46.9 1.1 %project.1 = bf16[32,32,128]{2,1,0:T(8,128)(2,1)} custom-call(bf16[32,40,128]{2,1,0:T(8,128)(2,1)S(1)} %all-to-all-done.packed), custom_call_target="tpu_custom_call" | custom-call | flops 20000000000 | bytes 262144 | tf_op jit(solution)/shard_map/project/pallas_call | solution.py:154
  47.9 3.9 %all-to-all-start.1 = ((bf16[32,32,128]{2,1,0:T(8,128)(2,1)}), bf16[32,32,128]{2,1,0:T(8,128)(2,1)S(1)}, u32[]{:S(2)}, u32[]{:S(2)}) async-start(bf16[32,32,128]{2,1,0:T(8,128)(2,1)} %project.1), calls=%async_computation.1 | async-start | bytes 524288 | tf_op jit(solution)/shard_map/all_to_all | solution.py:362
  51.8 0.0 collective-permute-done.3.refs_3_
  51.8 0.0 collective-permute-done.2.refs_2_
  51.8 0.0 copy-start
  51.8 0.8 copy-done
  52.6 0.0 collective-permute-done.1.refs_1_
  52.6 0.0 copy-start.2
  52.6 0.8 copy-done.2
  53.4 0.0 copy-start.1
  53.4 1.0 %copy-done.1 = bf16[2112,128]{1,0:T(8,128)(2,1)S(1)} copy-done((bf16[2112,128]{1,0:T(8,128)(2,1)S(1)}, bf16[2112,128]{1,0:T(8,128)(2,1)}, u32[]{:S(2)}) %copy-start.1) | copy-done | bytes 540696
  54.5 0.0 copy-start.3
  54.5 1.0 %copy-done.3 = bf16[2112,128]{1,0:T(8,128)(2,1)S(1)} copy-done((bf16[2112,128]{1,0:T(8,128)(2,1)S(1)}, bf16[2112,128]{1,0:T(8,128)(2,1)}, u32[]{:S(2)}) %copy-start.3) | copy-done | bytes 540696
  55.5 0.1 all_four.1.refs_0_.refs_1_
  55.7 1.9 %collective-permute-start.4 = (bf16[8448,128]{1,0:T(8,128)(2,1)S(1)}, bf16[8448,128]{1,0:T(8,128)(2,1)}, u32[]{:S(2)}, u32[]{:S(2)}) collective-permute-start(bf16[8448,128]{1,0:T(8,128)(2,1)S(1)} %all_four.1.refs_0_.refs_1_), channel_id=1, source_target_pairs={{0,32},{32,0},{64,96},{96,64},{128,160},{160,128},{192,224},{224,1... | collective-permute-start | bytes 6488072 | tf_op jit(solution)/shard_map/ppermute | solution.py:361
  57.6 16.2 %all-to-all-done.1 = bf16[32,32,128]{2,1,0:T(8,128)(2,1)S(1)} async-done(((bf16[32,32,128]{2,1,0:T(8,128)(2,1)}), bf16[32,32,128]{2,1,0:T(8,128)(2,1)S(1)}, u32[]{:S(2)}, u32[]{:S(2)}) %all-to-all-start.1) | async-done | bytes 262176 | tf_op jit(solution)/shard_map/all_to_all | solution.py:362
  73.8 0.1 turn.1.turned
  73.9 0.0 collective-permute-done.4.refs_2_.refs_3_
  74.0 10.9 %score.1 = f32[32,128]{1,0:T(8,128)S(1)} custom-call(s32[1]{0:T(128)} %bitcast.group, bf16[128,1024]{1,0:T(8,128)(2,1)S(1)} %turn.1.turned, bf16[8448,128]{1,0:T(8,128)(2,1)S(1)} %all_four.1.refs_0_.refs_1_, bf16[8448,128]{1,0:T(8,128)(2,1)S(1)} %all_four.1.refs_0_.refs_1_, bf16[8448,128]{1,0:T(8,128)(2,1)} %collective-permute-done.4.refs_2_.refs_3_, ...), custom_call_target="tpu_custom_call" | custom-call | flops 40000000000 | bytes 4325376 | tf_op jit(solution)/shard_map/score/pallas_call | solution.py:233
  84.9 16.3 %all_to_all.15 = f32[32,1,128]{2,1,0:T(1,128)S(1)} all-to-all(f32[32,1,128]{2,1,0:T(1,128)S(1)} %bitcast.13), channel_id=1, replica_groups=mesh['blk'=16,'shard'=32] {'shard'}, dimensions={0} | all-to-all | bytes 32768 | tf_op jit(solution)/shard_map/all_to_all | solution.py:364
  101.2 1.3 %select.1 = f32[1,128]{1,0:T(1,128)} custom-call(f32[32,128]{1,0:T(8,128)S(1)} %bitcast.12), custom_call_target="tpu_custom_call" | custom-call | tf_op jit(solution)/shard_map/select/pallas_call | solution.py:331
  (1 shorter events, 0.0 us)
Async XLA Ops:
  1.9 20.7 %collective-permute-start = (bf16[1056,128]{1,0:T(8,128)(2,1)}, bf16[1056,128]{1,0:T(8,128)(2,1)S(1)}, u32[]{:S(2)}, u32[]{:S(2)}) collective-permute-start(bf16[1056,128]{1,0:T(8,128)(2,1)} %get-tuple-element.8.own), channel_id=1, source_target_pairs={{0,64},{32,96},{64,0},{96,32},{128,192},{160,224},{192,128},{224,1... | collective-permute-start | bytes 811016 | tf_op jit(solution)/shard_map/ppermute | solution.py:356
  7.0 39.8 %all-to-all-start = ((bf16[32,40,128]{2,1,0:T(8,128)(2,1)}), bf16[32,40,128]{2,1,0:T(8,128)(2,1)S(1)}, u32[]{:S(2)}, u32[]{:S(2)}) async-start(bf16[32,40,128]{2,1,0:T(8,128)(2,1)} %get-tuple-element.7), calls=%async_computation | async-start | bytes 655360 | tf_op jit(solution)/shard_map/all_to_all | solution.py:359
  22.6 1.0 copy-start.4
  23.6 28.2 %collective-permute-start.3 = (bf16[2112,128]{1,0:T(8,128)(2,1)S(1)}, bf16[2112,128]{1,0:T(8,128)(2,1)S(1)}, u32[]{:S(2)}, u32[]{:S(2)}) collective-permute-start(bf16[2112,128]{1,0:T(8,128)(2,1)S(1)} %both.1.refs_0_), channel_id=1, source_target_pairs={{0,256},{32,288},{64,320},{96,352},{128,384},{160,416},{192,448},{... | collective-permute-start | bytes 1622024 | tf_op jit(solution)/shard_map/ppermute | solution.py:358
  26.1 25.8 %collective-permute-start.2 = (bf16[2112,128]{1,0:T(8,128)(2,1)S(1)}, bf16[2112,128]{1,0:T(8,128)(2,1)S(1)}, u32[]{:S(2)}, u32[]{:S(2)}) collective-permute-start(bf16[2112,128]{1,0:T(8,128)(2,1)S(1)} %both.1.refs_0_), channel_id=1, source_target_pairs={{0,384},{32,416},{64,448},{96,480},{128,0},{160,32},{192,64},{224,... | collective-permute-start | bytes 1622024 | tf_op jit(solution)/shard_map/ppermute | solution.py:358
  30.1 22.5 %collective-permute-start.1 = (bf16[2112,128]{1,0:T(8,128)(2,1)S(1)}, bf16[2112,128]{1,0:T(8,128)(2,1)S(1)}, u32[]{:S(2)}, u32[]{:S(2)}) collective-permute-start(bf16[2112,128]{1,0:T(8,128)(2,1)S(1)} %both.1.refs_0_), channel_id=1, source_target_pairs={{0,128},{32,160},{64,192},{96,224},{128,256},{160,288},{192,320},{... | collective-permute-start | bytes 1622024 | tf_op jit(solution)/shard_map/ppermute | solution.py:358
  47.9 25.9 %all-to-all-start.1 = ((bf16[32,32,128]{2,1,0:T(8,128)(2,1)}), bf16[32,32,128]{2,1,0:T(8,128)(2,1)S(1)}, u32[]{:S(2)}, u32[]{:S(2)}) async-start(bf16[32,32,128]{2,1,0:T(8,128)(2,1)} %project.1), calls=%async_computation.1 | async-start | bytes 524288 | tf_op jit(solution)/shard_map/all_to_all | solution.py:362
  51.8 0.8 copy-start
  52.6 0.8 copy-start.2
  53.4 1.0 %copy-start.1 = (bf16[2112,128]{1,0:T(8,128)(2,1)S(1)}, bf16[2112,128]{1,0:T(8,128)(2,1)}, u32[]{:S(2)}) copy-start(bf16[2112,128]{1,0:T(8,128)(2,1)} %copy-done) | copy-start | bytes 1622020
  54.5 1.0 %copy-start.3 = (bf16[2112,128]{1,0:T(8,128)(2,1)S(1)}, bf16[2112,128]{1,0:T(8,128)(2,1)}, u32[]{:S(2)}) copy-start(bf16[2112,128]{1,0:T(8,128)(2,1)} %copy-done.2) | copy-start | bytes 1622020
  55.7 18.3 %collective-permute-start.4 = (bf16[8448,128]{1,0:T(8,128)(2,1)S(1)}, bf16[8448,128]{1,0:T(8,128)(2,1)}, u32[]{:S(2)}, u32[]{:S(2)}) collective-permute-start(bf16[8448,128]{1,0:T(8,128)(2,1)S(1)} %all_four.1.refs_0_.refs_1_), channel_id=1, source_target_pairs={{0,32},{32,0},{64,96},{96,64},{128,160},{160,128},{192,224},{224,1... | collective-permute-start | bytes 6488072 | tf_op jit(solution)/shard_map/ppermute | solution.py:361

commit v4 on v3

--- a/solution.py
+++ b/solution.py
@@ -20,9 +20,11 @@
 STOCK_ROWS = P_DEV * PT
 MASK_ROWS = P_DEV * QUERIES // 128
 ROWS = STOCK_ROWS + MASK_ROWS
-STEPS = GROUPS // 4
+STEPS = 2
+SIDES = GROUPS // STEPS
 FOLD = 128 // QT
 FOLD_ROWS = HID_DEV // FOLD
+FIRST = 8
 
 
 def vmem():
@@ -67,7 +69,7 @@
                     moved = pltpu.roll(bands[c], (QT * (c - k)) % 128, 1)
                     folded = jnp.where(slot == c, moved, folded)
             both = jnp.concatenate([folded, weight_rows], axis=0)
-            out[tile * FOLD + k] = both.astype(jnp.bfloat16)
+            out[(tile * FOLD + k - FIRST) % LANES] = both.astype(jnp.bfloat16)
 
 
 def prepare_kernel(hidden, weight, passages, cands, counts, permitted, packed, own):
@@ -191,7 +193,7 @@
 
 
 def score_kernel(group, turned, *refs):
-    blocks, (out, best, masks) = refs[:4], refs[4:]
+    blocks, (out, best, masks) = refs[:SIDES], refs[SIDES:]
     step = pl.program_id(0)
 
     quarter = group[0] // FOLD
@@ -218,7 +220,8 @@
             scores = scores + lax.dot_general(
                 member, part, (((1,), (1,)), ((), ())), preferred_element_type=jnp.float32
             )
-        wanted = (group[0] % FOLD) * QT + row_index((QT, 128))
+        lane = lax.rem(row_index((LANES, 128)) + FIRST, LANES)
+        wanted = (group[0] % FOLD) * LANES + lane
         chosen = (lane_index((QT, 128)) == wanted).astype(jnp.bfloat16)
         live = lax.dot_general(
             chosen,
@@ -237,19 +240,23 @@
         in_specs=[
             pl.BlockSpec(memory_space=pltpu.SMEM),
             pl.BlockSpec((DIM, TOK), lambda i: (0, 0)),
-            *[pl.BlockSpec((ROWS, DIM), lambda i, at=at: (i + at, 0)) for at in (0, STEPS)] * 2,
+            *[
+                pl.BlockSpec((ROWS, DIM), lambda i, at=at: (i + at * STEPS, 0))
+                for at in range(SIDES // 2)
+            ]
+            * 2,
         ],
         out_specs=pl.BlockSpec((QT, GROUPS * P_DEV), lambda i: (0, 0)),
         scratch_shapes=[
-            pltpu.VMEM((4, STEPS, P_DEV, TOK), jnp.float32),
-            pltpu.VMEM((4, STEPS, P_DEV, 128), jnp.float32),
+            pltpu.VMEM((SIDES, STEPS, P_DEV, TOK), jnp.float32),
+            pltpu.VMEM((SIDES, STEPS, P_DEV, 128), jnp.float32),
         ],
         cost_estimate=pl.CostEstimate(
             flops=40 * 10**9, bytes_accessed=GROUPS * ROWS * DIM * 2, transcendentals=0
         ),
         compiler_params=limit(16),
         name="score",
-    )(group, queries, mine, mine, theirs, theirs)
+    )(group, queries, *[mine] * (SIDES // 2), *[theirs] * (SIDES // 2))
 
 
 def split_exchange(arrays, distance):
@@ -338,6 +345,11 @@
     )(table)
 
 
+def exchanged(blocks):
+    order = [(FIRST + k) % LANES for k in range(LANES)]
+    return lax.all_to_all(blocks, "shard", 0, 0, tiled=True, axis_index_groups=[order])
+
+
 def turned(steps):
     return [(i, (i + steps) % GROUPS) for i in range(GROUPS)]
 
@@ -356,12 +368,12 @@
     across = lax.ppermute(own, "blk", [(i, i ^ 2) for i in range(GROUPS)])
     pair = both(own, across)
     along_x = [lax.ppermute(pair, "blk", turned(4 * x)) for x in (1, 3, 2)]
-    rows = project(lax.all_to_all(packed, "shard", 0, 0, tiled=True))
+    rows = project(exchanged(packed))
     mine = all_four(pair, *along_x)
     theirs = lax.ppermute(mine, "blk", [(i, i ^ 1) for i in range(GROUPS)])
-    queries = lax.all_to_all(rows, "shard", 0, 0, tiled=True).reshape(TOK, DIM)
+    queries = exchanged(rows).reshape(TOK, DIM)
     table = score(group, turn(queries), mine, theirs)
-    entries = lax.all_to_all(table.reshape(LANES, 1, 128), "shard", 0, 0, tiled=True)
+    entries = exchanged(table.reshape(LANES, 1, 128))
     return select(entries.reshape(LANES, 128))
 
 

time: 103 us -> 95.8 us (0.930)
  waiting for transfers between devices: 31 us -> 12.2 us
  starting transfers between devices: 34.9 us -> 47.2 us
    all_to_all x2, waiting for transfers between devices: 31 us -> 12.2 us  [exchanged(): lax.all_to_all(blocks, 'shard', 0, 0, tiled=True, axis_index_groups=[order])]
    all_to_all x2, starting transfers between devices: 19.5 us -> 31.8 us  [exchanged(): lax.all_to_all(blocks, 'shard', 0, 0, tiled=True, axis_index_groups=[order])]
where the time goes in v4:
time: 95.8 us; the launch traced here: 95.3 us
  starting transfers between devices  47.2 us (49%)
  blocking collectives  15.7 us (16%)
  Pallas kernels  15.3 us (16%)
  waiting for transfers between devices  12.2 us (13%)
  local copies, waits for them, and re-layouts  4.63 us (5%)
    all_to_all x2, starting transfers between devices, exchanged(): lax.all_to_all(blocks, 'shard', 0, 0, tiled=True, axis_index_groups=[order])  31.8 us
    all_to_all x1, blocking collectives, exchanged(): lax.all_to_all(blocks, 'shard', 0, 0, tiled=True, axis_index_groups=[order])  15.7 us
    all_to_all x2, waiting for transfers between devices, exchanged(): lax.all_to_all(blocks, 'shard', 0, 0, tiled=True, axis_index_groups=[order])  12.2 us
    pallas_call x1, Pallas kernels, score(): pl.pallas_call(score_kernel, out_shape=jax.ShapeDtypeStruct((QT, GROUPS *...  10.8 us
    ppermute x3, starting transfers between devices, body(): along_x = [lax.ppermute(pair, 'blk', turned(4 * x)) for x in (1, 3, 2)]  8.4 us
    ppermute x1, starting transfers between devices, body(): across = lax.ppermute(own, 'blk', [(i, i ^ 2) for i in range(GROUPS)])  5.09 us
    unnamed x10, local copies, waits for them, and re-layouts  4.63 us
    ppermute x1, starting transfers between devices, body(): theirs = lax.ppermute(mine, 'blk', [(i, i ^ 1) for i in range(GROUPS)])  1.92 us
  transfers between devices with their start and end apart: 7, of which 2 were waited for; matrix products, arithmetic and copies ran while one was open for 0% of the time, Pallas kernels for 1%

profile of v4, /device:TPU:4, one launch (start us, length us, event | category | flops | bytes accessed | tf_op | source)
XLA Modules:
  0.0 95.3 jit_solution(10205074480488276692)
XLA Ops:
  0.0 1.9 %prepare.1 = (bf16[32,40,128]{2,1,0:T(8,128)(2,1)}, bf16[1056,128]{1,0:T(8,128)(2,1)}) custom-call(bf16[32,1024]{1,0:T(8,128)(2,1)} %hidden.1, bf16[32,128]{1,0:T(8,128)(2,1)} %weight.1, bf16[1024,128]{1,0:T(8,128)(2,1)} %bitcast.14, s32[4,512]{1,0:T(4,128)} %bitcast.15, s32[1,512]{1,0:T(1,128)} %bitcast.16, s32[1,512]{1,0:T(1,128)} %permitted.1), custom_call_target="tpu_custom_call" | custom-call | tf_op jit(solution)/shard_map/prepare/pallas_call | solution.py:81
  1.9 5.1 %collective-permute-start = (bf16[1056,128]{1,0:T(8,128)(2,1)}, bf16[1056,128]{1,0:T(8,128)(2,1)S(1)}, u32[]{:S(2)}, u32[]{:S(2)}) collective-permute-start(bf16[1056,128]{1,0:T(8,128)(2,1)} %get-tuple-element.8.own), channel_id=1, source_target_pairs={{0,64},{32,96},{64,0},{96,32},{128,192},{160,224},{192,128},{224,1... | collective-permute-start | bytes 811016 | tf_op jit(solution)/shard_map/ppermute | solution.py:368
  7.0 19.2 %all-to-all-start = ((bf16[32,40,128]{2,1,0:T(8,128)(2,1)}), bf16[32,40,128]{2,1,0:T(8,128)(2,1)S(1)}, u32[]{:S(2)}, u32[]{:S(2)}) async-start(bf16[32,40,128]{2,1,0:T(8,128)(2,1)} %get-tuple-element.7), calls=%async_computation | async-start | bytes 655360 | tf_op jit(solution)/shard_map/all_to_all | solution.py:350
  26.2 0.0 collective-permute-done.across
  26.2 0.0 copy-start.4
  26.2 0.9 copy-done.4
  27.2 2.4 %collective-permute-start.3 = (bf16[2112,128]{1,0:T(8,128)(2,1)S(1)}, bf16[2112,128]{1,0:T(8,128)(2,1)S(1)}, u32[]{:S(2)}, u32[]{:S(2)}) collective-permute-start(bf16[2112,128]{1,0:T(8,128)(2,1)S(1)} %both.1.refs_0_), channel_id=1, source_target_pairs={{0,256},{32,288},{64,320},{96,352},{128,384},{160,416},{192,448},{... | collective-permute-start | bytes 1622024 | tf_op jit(solution)/shard_map/ppermute | solution.py:370
  29.6 4.1 %collective-permute-start.2 = (bf16[2112,128]{1,0:T(8,128)(2,1)S(1)}, bf16[2112,128]{1,0:T(8,128)(2,1)S(1)}, u32[]{:S(2)}, u32[]{:S(2)}) collective-permute-start(bf16[2112,128]{1,0:T(8,128)(2,1)S(1)} %both.1.refs_0_), channel_id=1, source_target_pairs={{0,384},{32,416},{64,448},{96,480},{128,0},{160,32},{192,64},{224,... | collective-permute-start | bytes 1622024 | tf_op jit(solution)/shard_map/ppermute | solution.py:370
  33.7 1.9 %collective-permute-start.1 = (bf16[2112,128]{1,0:T(8,128)(2,1)S(1)}, bf16[2112,128]{1,0:T(8,128)(2,1)S(1)}, u32[]{:S(2)}, u32[]{:S(2)}) collective-permute-start(bf16[2112,128]{1,0:T(8,128)(2,1)S(1)} %both.1.refs_0_), channel_id=1, source_target_pairs={{0,128},{32,160},{64,192},{96,224},{128,256},{160,288},{192,320},{... | collective-permute-start | bytes 1622024 | tf_op jit(solution)/shard_map/ppermute | solution.py:370
  35.6 5.5 %all-to-all-done.packed = bf16[32,40,128]{2,1,0:T(8,128)(2,1)S(1)} async-done(((bf16[32,40,128]{2,1,0:T(8,128)(2,1)}), bf16[32,40,128]{2,1,0:T(8,128)(2,1)S(1)}, u32[]{:S(2)}, u32[]{:S(2)}) %all-to-all-start) | async-done | bytes 327712 | tf_op jit(solution)/shard_map/all_to_all | solution.py:350
  41.1 1.1 %project.1 = bf16[32,32,128]{2,1,0:T(8,128)(2,1)} custom-call(bf16[32,40,128]{2,1,0:T(8,128)(2,1)S(1)} %all-to-all-done.packed), custom_call_target="tpu_custom_call" | custom-call | flops 20000000000 | bytes 262144 | tf_op jit(solution)/shard_map/project/pallas_call | solution.py:156
  42.2 12.7 %all-to-all-start.1 = ((bf16[32,32,128]{2,1,0:T(8,128)(2,1)}), bf16[32,32,128]{2,1,0:T(8,128)(2,1)S(1)}, u32[]{:S(2)}, u32[]{:S(2)}) async-start(bf16[32,32,128]{2,1,0:T(8,128)(2,1)} %project.1), calls=%async_computation.1 | async-start | bytes 524288 | tf_op jit(solution)/shard_map/all_to_all | solution.py:350
  54.9 0.0 collective-permute-done.3.refs_3_
  54.9 0.0 collective-permute-done.2.refs_2_
  54.9 0.0 copy-start
  54.9 0.8 copy-done
  55.7 0.0 collective-permute-done.1.refs_1_
  55.7 0.0 copy-start.2
  55.7 0.8 copy-done.2
  56.5 0.0 copy-start.1
  56.5 1.0 %copy-done.1 = bf16[2112,128]{1,0:T(8,128)(2,1)S(1)} copy-done((bf16[2112,128]{1,0:T(8,128)(2,1)S(1)}, bf16[2112,128]{1,0:T(8,128)(2,1)}, u32[]{:S(2)}) %copy-start.1) | copy-done | bytes 540696
  57.5 0.0 copy-start.3
  57.5 1.0 %copy-done.3 = bf16[2112,128]{1,0:T(8,128)(2,1)S(1)} copy-done((bf16[2112,128]{1,0:T(8,128)(2,1)S(1)}, bf16[2112,128]{1,0:T(8,128)(2,1)}, u32[]{:S(2)}) %copy-start.3) | copy-done | bytes 540696
  58.6 0.1 all_four.1.refs_0_.refs_1_.refs_2_.refs_3_
  58.7 1.9 %collective-permute-start.4 = (bf16[8448,128]{1,0:T(8,128)(2,1)S(1)}, bf16[8448,128]{1,0:T(8,128)(2,1)}, u32[]{:S(2)}, u32[]{:S(2)}) collective-permute-start(bf16[8448,128]{1,0:T(8,128)(2,1)S(1)} %all_four.1.refs_0_.refs_1_.refs_2_.refs_3_), channel_id=1, source_target_pairs={{0,32},{32,0},{64,96},{96,64},{128,160},{160,128},{192,224},{224,1... | collective-permute-start | bytes 6488072 | tf_op jit(solution)/shard_map/ppermute | solution.py:373
  60.7 6.6 %all-to-all-done.1 = bf16[32,32,128]{2,1,0:T(8,128)(2,1)S(1)} async-done(((bf16[32,32,128]{2,1,0:T(8,128)(2,1)}), bf16[32,32,128]{2,1,0:T(8,128)(2,1)S(1)}, u32[]{:S(2)}, u32[]{:S(2)}) %all-to-all-start.1) | async-done | bytes 262176 | tf_op jit(solution)/shard_map/all_to_all | solution.py:350
  67.3 0.1 turn.1.turned
  67.5 0.0 collective-permute-done.4.refs_4_.refs_5_.refs_6_.refs_7_
  67.5 10.8 %score.1 = f32[32,128]{1,0:T(8,128)S(1)} custom-call(s32[1]{0:T(128)} %bitcast.group, bf16[128,1024]{1,0:T(8,128)(2,1)S(1)} %turn.1.turned, bf16[8448,128]{1,0:T(8,128)(2,1)S(1)} %all_four.1.refs_0_.refs_1_.refs_2_.refs_3_, bf16[8448,128]{1,0:T(8,128)(2,1)S(1)} %all_four.1.refs_0_.refs_1_.refs_2_.refs_3_, ...), custom_call_target="tpu_custom_call" | custom-call | flops 40000000000 | bytes 4325376 | tf_op jit(solution)/shard_map/score/pallas_call | solution.py:236
  78.2 15.7 %all_to_all.15 = f32[32,1,128]{2,1,0:T(1,128)S(1)} all-to-all(f32[32,1,128]{2,1,0:T(1,128)S(1)} %bitcast.13), channel_id=1, replica_groups={{8,9,10,11,12,13,14,15,16,17,18,19,20,21,22,23,24,25,26,27,28,29,30,31,..., dimensions={0} | all-to-all | bytes 32768 | tf_op jit(solution)/shard_map/all_to_all | solution.py:350
  93.9 1.3 %select.1 = f32[1,128]{1,0:T(1,128)} custom-call(f32[32,128]{1,0:T(8,128)S(1)} %bitcast.12), custom_call_target="tpu_custom_call" | custom-call | tf_op jit(solution)/shard_map/select/pallas_call | solution.py:338
  (1 shorter events, 0.0 us)
Async XLA Ops:
  1.9 24.3 %collective-permute-start = (bf16[1056,128]{1,0:T(8,128)(2,1)}, bf16[1056,128]{1,0:T(8,128)(2,1)S(1)}, u32[]{:S(2)}, u32[]{:S(2)}) collective-permute-start(bf16[1056,128]{1,0:T(8,128)(2,1)} %get-tuple-element.8.own), channel_id=1, source_target_pairs={{0,64},{32,96},{64,0},{96,32},{128,192},{160,224},{192,128},{224,1... | collective-permute-start | bytes 811016 | tf_op jit(solution)/shard_map/ppermute | solution.py:368
  7.0 34.1 %all-to-all-start = ((bf16[32,40,128]{2,1,0:T(8,128)(2,1)}), bf16[32,40,128]{2,1,0:T(8,128)(2,1)S(1)}, u32[]{:S(2)}, u32[]{:S(2)}) async-start(bf16[32,40,128]{2,1,0:T(8,128)(2,1)} %get-tuple-element.7), calls=%async_computation | async-start | bytes 655360 | tf_op jit(solution)/shard_map/all_to_all | solution.py:350
  26.2 1.0 %copy-start.4 = (bf16[1056,128]{1,0:T(8,128)(2,1)S(1)}, bf16[1056,128]{1,0:T(8,128)(2,1)}, u32[]{:S(2)}) copy-start(bf16[1056,128]{1,0:T(8,128)(2,1)} %get-tuple-element.8.own) | copy-start | bytes 811012
  27.2 27.7 %collective-permute-start.3 = (bf16[2112,128]{1,0:T(8,128)(2,1)S(1)}, bf16[2112,128]{1,0:T(8,128)(2,1)S(1)}, u32[]{:S(2)}, u32[]{:S(2)}) collective-permute-start(bf16[2112,128]{1,0:T(8,128)(2,1)S(1)} %both.1.refs_0_), channel_id=1, source_target_pairs={{0,256},{32,288},{64,320},{96,352},{128,384},{160,416},{192,448},{... | collective-permute-start | bytes 1622024 | tf_op jit(solution)/shard_map/ppermute | solution.py:370
  29.6 25.3 %collective-permute-start.2 = (bf16[2112,128]{1,0:T(8,128)(2,1)S(1)}, bf16[2112,128]{1,0:T(8,128)(2,1)S(1)}, u32[]{:S(2)}, u32[]{:S(2)}) collective-permute-start(bf16[2112,128]{1,0:T(8,128)(2,1)S(1)} %both.1.refs_0_), channel_id=1, source_target_pairs={{0,384},{32,416},{64,448},{96,480},{128,0},{160,32},{192,64},{224,... | collective-permute-start | bytes 1622024 | tf_op jit(solution)/shard_map/ppermute | solution.py:370
  33.7 22.0 %collective-permute-start.1 = (bf16[2112,128]{1,0:T(8,128)(2,1)S(1)}, bf16[2112,128]{1,0:T(8,128)(2,1)S(1)}, u32[]{:S(2)}, u32[]{:S(2)}) collective-permute-start(bf16[2112,128]{1,0:T(8,128)(2,1)S(1)} %both.1.refs_0_), channel_id=1, source_target_pairs={{0,128},{32,160},{64,192},{96,224},{128,256},{160,288},{192,320},{... | collective-permute-start | bytes 1622024 | tf_op jit(solution)/shard_map/ppermute | solution.py:370
  42.2 25.1 %all-to-all-start.1 = ((bf16[32,32,128]{2,1,0:T(8,128)(2,1)}), bf16[32,32,128]{2,1,0:T(8,128)(2,1)S(1)}, u32[]{:S(2)}, u32[]{:S(2)}) async-start(bf16[32,32,128]{2,1,0:T(8,128)(2,1)} %project.1), calls=%async_computation.1 | async-start | bytes 524288 | tf_op jit(solution)/shard_map/all_to_all | solution.py:350
  54.9 0.8 copy-start
  55.7 0.8 copy-start.2
  56.5 1.0 %copy-start.1 = (bf16[2112,128]{1,0:T(8,128)(2,1)S(1)}, bf16[2112,128]{1,0:T(8,128)(2,1)}, u32[]{:S(2)}) copy-start(bf16[2112,128]{1,0:T(8,128)(2,1)} %copy-done) | copy-start | bytes 1622020
  57.5 1.0 %copy-start.3 = (bf16[2112,128]{1,0:T(8,128)(2,1)S(1)}, bf16[2112,128]{1,0:T(8,128)(2,1)}, u32[]{:S(2)}) copy-start(bf16[2112,128]{1,0:T(8,128)(2,1)} %copy-done.2) | copy-start | bytes 1622020
  58.7 8.7 %collective-permute-start.4 = (bf16[8448,128]{1,0:T(8,128)(2,1)S(1)}, bf16[8448,128]{1,0:T(8,128)(2,1)}, u32[]{:S(2)}, u32[]{:S(2)}) collective-permute-start(bf16[8448,128]{1,0:T(8,128)(2,1)S(1)} %all_four.1.refs_0_.refs_1_.refs_2_.refs_3_), channel_id=1, source_target_pairs={{0,32},{32,0},{64,96},{96,64},{128,160},{160,128},{192,224},{224,1... | collective-permute-start | bytes 6488072 | tf_op jit(solution)/shard_map/ppermute | solution.py:373

commit v5 on v4

--- a/solution.py
+++ b/solution.py
@@ -25,6 +25,7 @@
 FOLD = 128 // QT
 FOLD_ROWS = HID_DEV // FOLD
 FIRST = 8
+FIRST_PACKED = 10
 
 
 def vmem():
@@ -69,7 +70,7 @@
                     moved = pltpu.roll(bands[c], (QT * (c - k)) % 128, 1)
                     folded = jnp.where(slot == c, moved, folded)
             both = jnp.concatenate([folded, weight_rows], axis=0)
-            out[(tile * FOLD + k - FIRST) % LANES] = both.astype(jnp.bfloat16)
+            out[(tile * FOLD + k - FIRST_PACKED) % LANES] = both.astype(jnp.bfloat16)
 
 
 def prepare_kernel(hidden, weight, passages, cands, counts, permitted, packed, own):
@@ -345,8 +346,8 @@
     )(table)
 
 
-def exchanged(blocks):
-    order = [(FIRST + k) % LANES for k in range(LANES)]
+def exchanged(blocks, first=FIRST):
+    order = [(first + k) % LANES for k in range(LANES)]
     return lax.all_to_all(blocks, "shard", 0, 0, tiled=True, axis_index_groups=[order])
 
 
@@ -368,7 +369,7 @@
     across = lax.ppermute(own, "blk", [(i, i ^ 2) for i in range(GROUPS)])
     pair = both(own, across)
     along_x = [lax.ppermute(pair, "blk", turned(4 * x)) for x in (1, 3, 2)]
-    rows = project(exchanged(packed))
+    rows = project(exchanged(packed, FIRST_PACKED))
     mine = all_four(pair, *along_x)
     theirs = lax.ppermute(mine, "blk", [(i, i ^ 1) for i in range(GROUPS)])
     queries = exchanged(rows).reshape(TOK, DIM)

time: 95.8 us -> 95.6 us (level)
  starting transfers between devices: 47.2 us -> 46 us
  waiting for transfers between devices: 12.2 us -> 13.4 us
    all_to_all x2, starting transfers between devices: 31.8 us -> 30.6 us  [exchanged(): lax.all_to_all(blocks, 'shard', 0, 0, tiled=True, axis_index_groups=[order])]
    all_to_all x2, waiting for transfers between devices: 12.2 us -> 13.3 us  [exchanged(): lax.all_to_all(blocks, 'shard', 0, 0, tiled=True, axis_index_groups=[order])]
where the time goes in v5:
time: 95.6 us; the launch traced here: 95 us
  starting transfers between devices  46 us (48%)
  blocking collectives  15.5 us (16%)
  Pallas kernels  15.3 us (16%)
  waiting for transfers between devices  13.4 us (14%)
  local copies, waits for them, and re-layouts  4.63 us (5%)
    all_to_all x2, starting transfers between devices, exchanged(): lax.all_to_all(blocks, 'shard', 0, 0, tiled=True, axis_index_groups=[order])  30.6 us
    all_to_all x1, blocking collectives, exchanged(): lax.all_to_all(blocks, 'shard', 0, 0, tiled=True, axis_index_groups=[order])  15.5 us
    all_to_all x2, waiting for transfers between devices, exchanged(): lax.all_to_all(blocks, 'shard', 0, 0, tiled=True, axis_index_groups=[order])  13.3 us
    pallas_call x1, Pallas kernels, score(): pl.pallas_call(score_kernel, out_shape=jax.ShapeDtypeStruct((QT, GROUPS *...  10.8 us
    ppermute x3, starting transfers between devices, body(): along_x = [lax.ppermute(pair, 'blk', turned(4 * x)) for x in (1, 3, 2)]  8.4 us
    ppermute x1, starting transfers between devices, body(): across = lax.ppermute(own, 'blk', [(i, i ^ 2) for i in range(GROUPS)])  5.09 us
    unnamed x10, local copies, waits for them, and re-layouts  4.63 us
    ppermute x1, starting transfers between devices, body(): theirs = lax.ppermute(mine, 'blk', [(i, i ^ 1) for i in range(GROUPS)])  1.92 us
  transfers between devices with their start and end apart: 7, of which 2 were waited for; matrix products, arithmetic and copies ran while one was open for 0% of the time, Pallas kernels for 1%

profile of v5, /device:TPU:4, one launch (start us, length us, event | category | flops | bytes accessed | tf_op | source)
XLA Modules:
  0.0 95.0 jit_solution(7977893476235338455)
XLA Ops:
  0.0 1.9 %prepare.1 = (bf16[32,40,128]{2,1,0:T(8,128)(2,1)}, bf16[1056,128]{1,0:T(8,128)(2,1)}) custom-call(bf16[32,1024]{1,0:T(8,128)(2,1)} %hidden.1, bf16[32,128]{1,0:T(8,128)(2,1)} %weight.1, bf16[1024,128]{1,0:T(8,128)(2,1)} %bitcast.14, s32[4,512]{1,0:T(4,128)} %bitcast.15, s32[1,512]{1,0:T(1,128)} %bitcast.16, s32[1,512]{1,0:T(1,128)} %permitted.1), custom_call_target="tpu_custom_call" | custom-call | tf_op jit(solution)/shard_map/prepare/pallas_call | solution.py:82
  1.9 5.1 %collective-permute-start = (bf16[1056,128]{1,0:T(8,128)(2,1)}, bf16[1056,128]{1,0:T(8,128)(2,1)S(1)}, u32[]{:S(2)}, u32[]{:S(2)}) collective-permute-start(bf16[1056,128]{1,0:T(8,128)(2,1)} %get-tuple-element.8.own), channel_id=1, source_target_pairs={{0,64},{32,96},{64,0},{96,32},{128,192},{160,224},{192,128},{224,1... | collective-permute-start | bytes 811016 | tf_op jit(solution)/shard_map/ppermute | solution.py:369
  7.0 17.4 %all-to-all-start = ((bf16[32,40,128]{2,1,0:T(8,128)(2,1)}), bf16[32,40,128]{2,1,0:T(8,128)(2,1)S(1)}, u32[]{:S(2)}, u32[]{:S(2)}) async-start(bf16[32,40,128]{2,1,0:T(8,128)(2,1)} %get-tuple-element.7), calls=%async_computation | async-start | bytes 655360 | tf_op jit(solution)/shard_map/all_to_all | solution.py:351
  24.4 0.0 collective-permute-done.across
  24.4 0.0 copy-start.4
  24.4 0.9 copy-done.4
  25.4 2.4 %collective-permute-start.3 = (bf16[2112,128]{1,0:T(8,128)(2,1)S(1)}, bf16[2112,128]{1,0:T(8,128)(2,1)S(1)}, u32[]{:S(2)}, u32[]{:S(2)}) collective-permute-start(bf16[2112,128]{1,0:T(8,128)(2,1)S(1)} %both.1.refs_0_), channel_id=1, source_target_pairs={{0,256},{32,288},{64,320},{96,352},{128,384},{160,416},{192,448},{... | collective-permute-start | bytes 1622024 | tf_op jit(solution)/shard_map/ppermute | solution.py:371
  27.8 4.1 %collective-permute-start.2 = (bf16[2112,128]{1,0:T(8,128)(2,1)S(1)}, bf16[2112,128]{1,0:T(8,128)(2,1)S(1)}, u32[]{:S(2)}, u32[]{:S(2)}) collective-permute-start(bf16[2112,128]{1,0:T(8,128)(2,1)S(1)} %both.1.refs_0_), channel_id=1, source_target_pairs={{0,384},{32,416},{64,448},{96,480},{128,0},{160,32},{192,64},{224,... | collective-permute-start | bytes 1622024 | tf_op jit(solution)/shard_map/ppermute | solution.py:371
  31.9 1.9 %collective-permute-start.1 = (bf16[2112,128]{1,0:T(8,128)(2,1)S(1)}, bf16[2112,128]{1,0:T(8,128)(2,1)S(1)}, u32[]{:S(2)}, u32[]{:S(2)}) collective-permute-start(bf16[2112,128]{1,0:T(8,128)(2,1)S(1)} %both.1.refs_0_), channel_id=1, source_target_pairs={{0,128},{32,160},{64,192},{96,224},{128,256},{160,288},{192,320},{... | collective-permute-start | bytes 1622024 | tf_op jit(solution)/shard_map/ppermute | solution.py:371
  33.8 6.7 %all-to-all-done.packed = bf16[32,40,128]{2,1,0:T(8,128)(2,1)S(1)} async-done(((bf16[32,40,128]{2,1,0:T(8,128)(2,1)}), bf16[32,40,128]{2,1,0:T(8,128)(2,1)S(1)}, u32[]{:S(2)}, u32[]{:S(2)}) %all-to-all-start) | async-done | bytes 327712 | tf_op jit(solution)/shard_map/all_to_all | solution.py:351
  40.5 1.1 %project.1 = bf16[32,32,128]{2,1,0:T(8,128)(2,1)} custom-call(bf16[32,40,128]{2,1,0:T(8,128)(2,1)S(1)} %all-to-all-done.packed), custom_call_target="tpu_custom_call" | custom-call | flops 20000000000 | bytes 262144 | tf_op jit(solution)/shard_map/project/pallas_call | solution.py:157
  41.6 13.3 %all-to-all-start.1 = ((bf16[32,32,128]{2,1,0:T(8,128)(2,1)}), bf16[32,32,128]{2,1,0:T(8,128)(2,1)S(1)}, u32[]{:S(2)}, u32[]{:S(2)}) async-start(bf16[32,32,128]{2,1,0:T(8,128)(2,1)} %project.1), calls=%async_computation.1 | async-start | bytes 524288 | tf_op jit(solution)/shard_map/all_to_all | solution.py:351
  54.9 0.0 collective-permute-done.3.refs_3_
  54.9 0.0 collective-permute-done.2.refs_2_
  54.9 0.0 copy-start
  54.9 0.8 copy-done
  55.7 0.0 collective-permute-done.1.refs_1_
  55.7 0.0 copy-start.2
  55.7 0.8 copy-done.2
  56.5 0.0 copy-start.1
  56.5 1.0 %copy-done.1 = bf16[2112,128]{1,0:T(8,128)(2,1)S(1)} copy-done((bf16[2112,128]{1,0:T(8,128)(2,1)S(1)}, bf16[2112,128]{1,0:T(8,128)(2,1)}, u32[]{:S(2)}) %copy-start.1) | copy-done | bytes 540696
  57.5 0.0 copy-start.3
  57.5 1.0 %copy-done.3 = bf16[2112,128]{1,0:T(8,128)(2,1)S(1)} copy-done((bf16[2112,128]{1,0:T(8,128)(2,1)S(1)}, bf16[2112,128]{1,0:T(8,128)(2,1)}, u32[]{:S(2)}) %copy-start.3) | copy-done | bytes 540696
  58.6 0.1 all_four.1.refs_0_.refs_1_.refs_2_.refs_3_
  58.7 1.9 %collective-permute-start.4 = (bf16[8448,128]{1,0:T(8,128)(2,1)S(1)}, bf16[8448,128]{1,0:T(8,128)(2,1)}, u32[]{:S(2)}, u32[]{:S(2)}) collective-permute-start(bf16[8448,128]{1,0:T(8,128)(2,1)S(1)} %all_four.1.refs_0_.refs_1_.refs_2_.refs_3_), channel_id=1, source_target_pairs={{0,32},{32,0},{64,96},{96,64},{128,160},{160,128},{192,224},{224,1... | collective-permute-start | bytes 6488072 | tf_op jit(solution)/shard_map/ppermute | solution.py:374
  60.7 6.6 %all-to-all-done.1 = bf16[32,32,128]{2,1,0:T(8,128)(2,1)S(1)} async-done(((bf16[32,32,128]{2,1,0:T(8,128)(2,1)}), bf16[32,32,128]{2,1,0:T(8,128)(2,1)S(1)}, u32[]{:S(2)}, u32[]{:S(2)}) %all-to-all-start.1) | async-done | bytes 262176 | tf_op jit(solution)/shard_map/all_to_all | solution.py:351
  67.3 0.1 turn.1.turned
  67.4 0.0 collective-permute-done.4.refs_4_.refs_5_.refs_6_.refs_7_
  67.4 10.8 %score.1 = f32[32,128]{1,0:T(8,128)S(1)} custom-call(s32[1]{0:T(128)} %bitcast.group, bf16[128,1024]{1,0:T(8,128)(2,1)S(1)} %turn.1.turned, bf16[8448,128]{1,0:T(8,128)(2,1)S(1)} %all_four.1.refs_0_.refs_1_.refs_2_.refs_3_, bf16[8448,128]{1,0:T(8,128)(2,1)S(1)} %all_four.1.refs_0_.refs_1_.refs_2_.refs_3_, ...), custom_call_target="tpu_custom_call" | custom-call | flops 40000000000 | bytes 4325376 | tf_op jit(solution)/shard_map/score/pallas_call | solution.py:237
  78.2 15.5 %all_to_all.15 = f32[32,1,128]{2,1,0:T(1,128)S(1)} all-to-all(f32[32,1,128]{2,1,0:T(1,128)S(1)} %bitcast.13), channel_id=1, replica_groups={{8,9,10,11,12,13,14,15,16,17,18,19,20,21,22,23,24,25,26,27,28,29,30,31,..., dimensions={0} | all-to-all | bytes 32768 | tf_op jit(solution)/shard_map/all_to_all | solution.py:351
  93.7 1.3 %select.1 = f32[1,128]{1,0:T(1,128)} custom-call(f32[32,128]{1,0:T(8,128)S(1)} %bitcast.12), custom_call_target="tpu_custom_call" | custom-call | tf_op jit(solution)/shard_map/select/pallas_call | solution.py:339
  (1 shorter events, 0.0 us)
Async XLA Ops:
  1.9 22.5 %collective-permute-start = (bf16[1056,128]{1,0:T(8,128)(2,1)}, bf16[1056,128]{1,0:T(8,128)(2,1)S(1)}, u32[]{:S(2)}, u32[]{:S(2)}) collective-permute-start(bf16[1056,128]{1,0:T(8,128)(2,1)} %get-tuple-element.8.own), channel_id=1, source_target_pairs={{0,64},{32,96},{64,0},{96,32},{128,192},{160,224},{192,128},{224,1... | collective-permute-start | bytes 811016 | tf_op jit(solution)/shard_map/ppermute | solution.py:369
  7.0 33.5 %all-to-all-start = ((bf16[32,40,128]{2,1,0:T(8,128)(2,1)}), bf16[32,40,128]{2,1,0:T(8,128)(2,1)S(1)}, u32[]{:S(2)}, u32[]{:S(2)}) async-start(bf16[32,40,128]{2,1,0:T(8,128)(2,1)} %get-tuple-element.7), calls=%async_computation | async-start | bytes 655360 | tf_op jit(solution)/shard_map/all_to_all | solution.py:351
  24.4 1.0 %copy-start.4 = (bf16[1056,128]{1,0:T(8,128)(2,1)S(1)}, bf16[1056,128]{1,0:T(8,128)(2,1)}, u32[]{:S(2)}) copy-start(bf16[1056,128]{1,0:T(8,128)(2,1)} %get-tuple-element.8.own) | copy-start | bytes 811012
  25.4 29.5 %collective-permute-start.3 = (bf16[2112,128]{1,0:T(8,128)(2,1)S(1)}, bf16[2112,128]{1,0:T(8,128)(2,1)S(1)}, u32[]{:S(2)}, u32[]{:S(2)}) collective-permute-start(bf16[2112,128]{1,0:T(8,128)(2,1)S(1)} %both.1.refs_0_), channel_id=1, source_target_pairs={{0,256},{32,288},{64,320},{96,352},{128,384},{160,416},{192,448},{... | collective-permute-start | bytes 1622024 | tf_op jit(solution)/shard_map/ppermute | solution.py:371
  27.8 27.1 %collective-permute-start.2 = (bf16[2112,128]{1,0:T(8,128)(2,1)S(1)}, bf16[2112,128]{1,0:T(8,128)(2,1)S(1)}, u32[]{:S(2)}, u32[]{:S(2)}) collective-permute-start(bf16[2112,128]{1,0:T(8,128)(2,1)S(1)} %both.1.refs_0_), channel_id=1, source_target_pairs={{0,384},{32,416},{64,448},{96,480},{128,0},{160,32},{192,64},{224,... | collective-permute-start | bytes 1622024 | tf_op jit(solution)/shard_map/ppermute | solution.py:371
  31.9 23.8 %collective-permute-start.1 = (bf16[2112,128]{1,0:T(8,128)(2,1)S(1)}, bf16[2112,128]{1,0:T(8,128)(2,1)S(1)}, u32[]{:S(2)}, u32[]{:S(2)}) collective-permute-start(bf16[2112,128]{1,0:T(8,128)(2,1)S(1)} %both.1.refs_0_), channel_id=1, source_target_pairs={{0,128},{32,160},{64,192},{96,224},{128,256},{160,288},{192,320},{... | collective-permute-start | bytes 1622024 | tf_op jit(solution)/shard_map/ppermute | solution.py:371
  41.6 25.7 %all-to-all-start.1 = ((bf16[32,32,128]{2,1,0:T(8,128)(2,1)}), bf16[32,32,128]{2,1,0:T(8,128)(2,1)S(1)}, u32[]{:S(2)}, u32[]{:S(2)}) async-start(bf16[32,32,128]{2,1,0:T(8,128)(2,1)} %project.1), calls=%async_computation.1 | async-start | bytes 524288 | tf_op jit(solution)/shard_map/all_to_all | solution.py:351
  54.9 0.8 copy-start
  55.7 0.8 copy-start.2
  56.5 1.0 %copy-start.1 = (bf16[2112,128]{1,0:T(8,128)(2,1)S(1)}, bf16[2112,128]{1,0:T(8,128)(2,1)}, u32[]{:S(2)}) copy-start(bf16[2112,128]{1,0:T(8,128)(2,1)} %copy-done) | copy-start | bytes 1622020
  57.5 1.0 %copy-start.3 = (bf16[2112,128]{1,0:T(8,128)(2,1)S(1)}, bf16[2112,128]{1,0:T(8,128)(2,1)}, u32[]{:S(2)}) copy-start(bf16[2112,128]{1,0:T(8,128)(2,1)} %copy-done.2) | copy-start | bytes 1622020
  58.7 8.7 %collective-permute-start.4 = (bf16[8448,128]{1,0:T(8,128)(2,1)S(1)}, bf16[8448,128]{1,0:T(8,128)(2,1)}, u32[]{:S(2)}, u32[]{:S(2)}) collective-permute-start(bf16[8448,128]{1,0:T(8,128)(2,1)S(1)} %all_four.1.refs_0_.refs_1_.refs_2_.refs_3_), channel_id=1, source_target_pairs={{0,32},{32,0},{64,96},{96,64},{128,160},{160,128},{192,224},{224,1... | collective-permute-start | bytes 6488072 | tf_op jit(solution)/shard_map/ppermute | solution.py:374

commit v6 on v4

--- a/solution.py
+++ b/solution.py
@@ -24,7 +24,7 @@
 SIDES = GROUPS // STEPS
 FOLD = 128 // QT
 FOLD_ROWS = HID_DEV // FOLD
-FIRST = 8
+FIRST = 10
 
 
 def vmem():

time: 95.8 us -> 95.6 us (level)
  starting transfers between devices: 47.2 us -> 44.3 us
  waiting for transfers between devices: 12.2 us -> 14.4 us
    all_to_all x2, starting transfers between devices: 31.8 us -> 28.9 us  [exchanged(): lax.all_to_all(blocks, 'shard', 0, 0, tiled=True, axis_index_groups=[order])]
    all_to_all x2, waiting for transfers between devices: 12.2 us -> 14.4 us  [exchanged(): lax.all_to_all(blocks, 'shard', 0, 0, tiled=True, axis_index_groups=[order])]
where the time goes in v6:
time: 95.6 us; the launch traced here: 95 us
  starting transfers between devices  44.3 us (46%)
  blocking collectives  16.1 us (17%)
  Pallas kernels  15.3 us (16%)
  waiting for transfers between devices  14.4 us (15%)
  local copies, waits for them, and re-layouts  4.63 us (5%)
    all_to_all x2, starting transfers between devices, exchanged(): lax.all_to_all(blocks, 'shard', 0, 0, tiled=True, axis_index_groups=[order])  28.9 us
    all_to_all x1, blocking collectives, exchanged(): lax.all_to_all(blocks, 'shard', 0, 0, tiled=True, axis_index_groups=[order])  16.1 us
    all_to_all x2, waiting for transfers between devices, exchanged(): lax.all_to_all(blocks, 'shard', 0, 0, tiled=True, axis_index_groups=[order])  14.4 us
    pallas_call x1, Pallas kernels, score(): pl.pallas_call(score_kernel, out_shape=jax.ShapeDtypeStruct((QT, GROUPS *...  10.7 us
    ppermute x3, starting transfers between devices, body(): along_x = [lax.ppermute(pair, 'blk', turned(4 * x)) for x in (1, 3, 2)]  8.4 us
    ppermute x1, starting transfers between devices, body(): across = lax.ppermute(own, 'blk', [(i, i ^ 2) for i in range(GROUPS)])  5.09 us
    unnamed x10, local copies, waits for them, and re-layouts  4.63 us
    ppermute x1, starting transfers between devices, body(): theirs = lax.ppermute(mine, 'blk', [(i, i ^ 1) for i in range(GROUPS)])  1.92 us
  transfers between devices with their start and end apart: 7, of which 2 were waited for; matrix products, arithmetic and copies ran while one was open for 0% of the time, Pallas kernels for 1%

profile of v6, /device:TPU:4, one launch (start us, length us, event | category | flops | bytes accessed | tf_op | source)
XLA Modules:
  0.0 95.0 jit_solution(10986243401975924707)
XLA Ops:
  0.0 1.9 %prepare.1 = (bf16[32,40,128]{2,1,0:T(8,128)(2,1)}, bf16[1056,128]{1,0:T(8,128)(2,1)}) custom-call(bf16[32,1024]{1,0:T(8,128)(2,1)} %hidden.1, bf16[32,128]{1,0:T(8,128)(2,1)} %weight.1, bf16[1024,128]{1,0:T(8,128)(2,1)} %bitcast.14, s32[4,512]{1,0:T(4,128)} %bitcast.15, s32[1,512]{1,0:T(1,128)} %bitcast.16, s32[1,512]{1,0:T(1,128)} %permitted.1), custom_call_target="tpu_custom_call" | custom-call | tf_op jit(solution)/shard_map/prepare/pallas_call | solution.py:81
  1.9 5.1 %collective-permute-start = (bf16[1056,128]{1,0:T(8,128)(2,1)}, bf16[1056,128]{1,0:T(8,128)(2,1)S(1)}, u32[]{:S(2)}, u32[]{:S(2)}) collective-permute-start(bf16[1056,128]{1,0:T(8,128)(2,1)} %get-tuple-element.8.own), channel_id=1, source_target_pairs={{0,64},{32,96},{64,0},{96,32},{128,192},{160,224},{192,128},{224,1... | collective-permute-start | bytes 811016 | tf_op jit(solution)/shard_map/ppermute | solution.py:368
  7.0 17.4 %all-to-all-start = ((bf16[32,40,128]{2,1,0:T(8,128)(2,1)}), bf16[32,40,128]{2,1,0:T(8,128)(2,1)S(1)}, u32[]{:S(2)}, u32[]{:S(2)}) async-start(bf16[32,40,128]{2,1,0:T(8,128)(2,1)} %get-tuple-element.7), calls=%async_computation | async-start | bytes 655360 | tf_op jit(solution)/shard_map/all_to_all | solution.py:350
  24.4 0.0 collective-permute-done.across
  24.4 0.0 copy-start.4
  24.4 0.9 copy-done.4
  25.4 2.4 %collective-permute-start.3 = (bf16[2112,128]{1,0:T(8,128)(2,1)S(1)}, bf16[2112,128]{1,0:T(8,128)(2,1)S(1)}, u32[]{:S(2)}, u32[]{:S(2)}) collective-permute-start(bf16[2112,128]{1,0:T(8,128)(2,1)S(1)} %both.1.refs_0_), channel_id=1, source_target_pairs={{0,256},{32,288},{64,320},{96,352},{128,384},{160,416},{192,448},{... | collective-permute-start | bytes 1622024 | tf_op jit(solution)/shard_map/ppermute | solution.py:370
  27.8 4.1 %collective-permute-start.2 = (bf16[2112,128]{1,0:T(8,128)(2,1)S(1)}, bf16[2112,128]{1,0:T(8,128)(2,1)S(1)}, u32[]{:S(2)}, u32[]{:S(2)}) collective-permute-start(bf16[2112,128]{1,0:T(8,128)(2,1)S(1)} %both.1.refs_0_), channel_id=1, source_target_pairs={{0,384},{32,416},{64,448},{96,480},{128,0},{160,32},{192,64},{224,... | collective-permute-start | bytes 1622024 | tf_op jit(solution)/shard_map/ppermute | solution.py:370
  31.9 1.9 %collective-permute-start.1 = (bf16[2112,128]{1,0:T(8,128)(2,1)S(1)}, bf16[2112,128]{1,0:T(8,128)(2,1)S(1)}, u32[]{:S(2)}, u32[]{:S(2)}) collective-permute-start(bf16[2112,128]{1,0:T(8,128)(2,1)S(1)} %both.1.refs_0_), channel_id=1, source_target_pairs={{0,128},{32,160},{64,192},{96,224},{128,256},{160,288},{192,320},{... | collective-permute-start | bytes 1622024 | tf_op jit(solution)/shard_map/ppermute | solution.py:370
  33.8 6.7 %all-to-all-done.packed = bf16[32,40,128]{2,1,0:T(8,128)(2,1)S(1)} async-done(((bf16[32,40,128]{2,1,0:T(8,128)(2,1)}), bf16[32,40,128]{2,1,0:T(8,128)(2,1)S(1)}, u32[]{:S(2)}, u32[]{:S(2)}) %all-to-all-start) | async-done | bytes 327712 | tf_op jit(solution)/shard_map/all_to_all | solution.py:350
  40.5 1.1 %project.1 = bf16[32,32,128]{2,1,0:T(8,128)(2,1)} custom-call(bf16[32,40,128]{2,1,0:T(8,128)(2,1)S(1)} %all-to-all-done.packed), custom_call_target="tpu_custom_call" | custom-call | flops 20000000000 | bytes 262144 | tf_op jit(solution)/shard_map/project/pallas_call | solution.py:156
  41.6 11.6 %all-to-all-start.1 = ((bf16[32,32,128]{2,1,0:T(8,128)(2,1)}), bf16[32,32,128]{2,1,0:T(8,128)(2,1)S(1)}, u32[]{:S(2)}, u32[]{:S(2)}) async-start(bf16[32,32,128]{2,1,0:T(8,128)(2,1)} %project.1), calls=%async_computation.1 | async-start | bytes 524288 | tf_op jit(solution)/shard_map/all_to_all | solution.py:350
  53.2 0.0 collective-permute-done.3.refs_3_
  53.2 0.0 collective-permute-done.2.refs_2_
  53.2 0.0 copy-start
  53.2 0.8 copy-done
  54.0 0.0 collective-permute-done.1.refs_1_
  54.0 0.0 copy-start.2
  54.0 0.8 copy-done.2
  54.8 0.0 copy-start.1
  54.8 1.0 %copy-done.1 = bf16[2112,128]{1,0:T(8,128)(2,1)S(1)} copy-done((bf16[2112,128]{1,0:T(8,128)(2,1)S(1)}, bf16[2112,128]{1,0:T(8,128)(2,1)}, u32[]{:S(2)}) %copy-start.1) | copy-done | bytes 540696
  55.9 0.0 copy-start.3
  55.9 1.0 %copy-done.3 = bf16[2112,128]{1,0:T(8,128)(2,1)S(1)} copy-done((bf16[2112,128]{1,0:T(8,128)(2,1)S(1)}, bf16[2112,128]{1,0:T(8,128)(2,1)}, u32[]{:S(2)}) %copy-start.3) | copy-done | bytes 540696
  56.9 0.1 all_four.1.refs_0_.refs_1_.refs_2_.refs_3_
  57.1 1.9 %collective-permute-start.4 = (bf16[8448,128]{1,0:T(8,128)(2,1)S(1)}, bf16[8448,128]{1,0:T(8,128)(2,1)}, u32[]{:S(2)}, u32[]{:S(2)}) collective-permute-start(bf16[8448,128]{1,0:T(8,128)(2,1)S(1)} %all_four.1.refs_0_.refs_1_.refs_2_.refs_3_), channel_id=1, source_target_pairs={{0,32},{32,0},{64,96},{96,64},{128,160},{160,128},{192,224},{224,1... | collective-permute-start | bytes 6488072 | tf_op jit(solution)/shard_map/ppermute | solution.py:373
  59.0 7.6 %all-to-all-done.1 = bf16[32,32,128]{2,1,0:T(8,128)(2,1)S(1)} async-done(((bf16[32,32,128]{2,1,0:T(8,128)(2,1)}), bf16[32,32,128]{2,1,0:T(8,128)(2,1)S(1)}, u32[]{:S(2)}, u32[]{:S(2)}) %all-to-all-start.1) | async-done | bytes 262176 | tf_op jit(solution)/shard_map/all_to_all | solution.py:350
  66.6 0.1 turn.1.turned
  66.8 0.0 collective-permute-done.4.refs_4_.refs_5_.refs_6_.refs_7_
  66.8 10.7 %score.1 = f32[32,128]{1,0:T(8,128)S(1)} custom-call(s32[1]{0:T(128)} %bitcast.group, bf16[128,1024]{1,0:T(8,128)(2,1)S(1)} %turn.1.turned, bf16[8448,128]{1,0:T(8,128)(2,1)S(1)} %all_four.1.refs_0_.refs_1_.refs_2_.refs_3_, bf16[8448,128]{1,0:T(8,128)(2,1)S(1)} %all_four.1.refs_0_.refs_1_.refs_2_.refs_3_, ...), custom_call_target="tpu_custom_call" | custom-call | flops 40000000000 | bytes 4325376 | tf_op jit(solution)/shard_map/score/pallas_call | solution.py:236
  77.5 16.1 %all_to_all.15 = f32[32,1,128]{2,1,0:T(1,128)S(1)} all-to-all(f32[32,1,128]{2,1,0:T(1,128)S(1)} %bitcast.13), channel_id=1, replica_groups={{10,11,12,13,14,15,16,17,18,19,20,21,22,23,24,25,26,27,28,29,30,31,0,1,..., dimensions={0} | all-to-all | bytes 32768 | tf_op jit(solution)/shard_map/all_to_all | solution.py:350
  93.7 1.3 %select.1 = f32[1,128]{1,0:T(1,128)} custom-call(f32[32,128]{1,0:T(8,128)S(1)} %bitcast.12), custom_call_target="tpu_custom_call" | custom-call | tf_op jit(solution)/shard_map/select/pallas_call | solution.py:338
  (1 shorter events, 0.0 us)
Async XLA Ops:
  1.9 22.5 %collective-permute-start = (bf16[1056,128]{1,0:T(8,128)(2,1)}, bf16[1056,128]{1,0:T(8,128)(2,1)S(1)}, u32[]{:S(2)}, u32[]{:S(2)}) collective-permute-start(bf16[1056,128]{1,0:T(8,128)(2,1)} %get-tuple-element.8.own), channel_id=1, source_target_pairs={{0,64},{32,96},{64,0},{96,32},{128,192},{160,224},{192,128},{224,1... | collective-permute-start | bytes 811016 | tf_op jit(solution)/shard_map/ppermute | solution.py:368
  7.0 33.5 %all-to-all-start = ((bf16[32,40,128]{2,1,0:T(8,128)(2,1)}), bf16[32,40,128]{2,1,0:T(8,128)(2,1)S(1)}, u32[]{:S(2)}, u32[]{:S(2)}) async-start(bf16[32,40,128]{2,1,0:T(8,128)(2,1)} %get-tuple-element.7), calls=%async_computation | async-start | bytes 655360 | tf_op jit(solution)/shard_map/all_to_all | solution.py:350
  24.4 1.0 %copy-start.4 = (bf16[1056,128]{1,0:T(8,128)(2,1)S(1)}, bf16[1056,128]{1,0:T(8,128)(2,1)}, u32[]{:S(2)}) copy-start(bf16[1056,128]{1,0:T(8,128)(2,1)} %get-tuple-element.8.own) | copy-start | bytes 811012
  25.4 27.8 %collective-permute-start.3 = (bf16[2112,128]{1,0:T(8,128)(2,1)S(1)}, bf16[2112,128]{1,0:T(8,128)(2,1)S(1)}, u32[]{:S(2)}, u32[]{:S(2)}) collective-permute-start(bf16[2112,128]{1,0:T(8,128)(2,1)S(1)} %both.1.refs_0_), channel_id=1, source_target_pairs={{0,256},{32,288},{64,320},{96,352},{128,384},{160,416},{192,448},{... | collective-permute-start | bytes 1622024 | tf_op jit(solution)/shard_map/ppermute | solution.py:370
  27.8 25.4 %collective-permute-start.2 = (bf16[2112,128]{1,0:T(8,128)(2,1)S(1)}, bf16[2112,128]{1,0:T(8,128)(2,1)S(1)}, u32[]{:S(2)}, u32[]{:S(2)}) collective-permute-start(bf16[2112,128]{1,0:T(8,128)(2,1)S(1)} %both.1.refs_0_), channel_id=1, source_target_pairs={{0,384},{32,416},{64,448},{96,480},{128,0},{160,32},{192,64},{224,... | collective-permute-start | bytes 1622024 | tf_op jit(solution)/shard_map/ppermute | solution.py:370
  31.9 22.2 %collective-permute-start.1 = (bf16[2112,128]{1,0:T(8,128)(2,1)S(1)}, bf16[2112,128]{1,0:T(8,128)(2,1)S(1)}, u32[]{:S(2)}, u32[]{:S(2)}) collective-permute-start(bf16[2112,128]{1,0:T(8,128)(2,1)S(1)} %both.1.refs_0_), channel_id=1, source_target_pairs={{0,128},{32,160},{64,192},{96,224},{128,256},{160,288},{192,320},{... | collective-permute-start | bytes 1622024 | tf_op jit(solution)/shard_map/ppermute | solution.py:370
  41.6 25.0 %all-to-all-start.1 = ((bf16[32,32,128]{2,1,0:T(8,128)(2,1)}), bf16[32,32,128]{2,1,0:T(8,128)(2,1)S(1)}, u32[]{:S(2)}, u32[]{:S(2)}) async-start(bf16[32,32,128]{2,1,0:T(8,128)(2,1)} %project.1), calls=%async_computation.1 | async-start | bytes 524288 | tf_op jit(solution)/shard_map/all_to_all | solution.py:350
  53.2 0.8 copy-start
  54.0 0.8 copy-start.2
  54.8 1.0 %copy-start.1 = (bf16[2112,128]{1,0:T(8,128)(2,1)S(1)}, bf16[2112,128]{1,0:T(8,128)(2,1)}, u32[]{:S(2)}) copy-start(bf16[2112,128]{1,0:T(8,128)(2,1)} %copy-done) | copy-start | bytes 1622020
  55.9 1.0 %copy-start.3 = (bf16[2112,128]{1,0:T(8,128)(2,1)S(1)}, bf16[2112,128]{1,0:T(8,128)(2,1)}, u32[]{:S(2)}) copy-start(bf16[2112,128]{1,0:T(8,128)(2,1)} %copy-done.2) | copy-start | bytes 1622020
  57.1 9.7 %collective-permute-start.4 = (bf16[8448,128]{1,0:T(8,128)(2,1)S(1)}, bf16[8448,128]{1,0:T(8,128)(2,1)}, u32[]{:S(2)}, u32[]{:S(2)}) collective-permute-start(bf16[8448,128]{1,0:T(8,128)(2,1)S(1)} %all_four.1.refs_0_.refs_1_.refs_2_.refs_3_), channel_id=1, source_target_pairs={{0,32},{32,0},{64,96},{96,64},{128,160},{160,128},{192,224},{224,1... | collective-permute-start | bytes 6488072 | tf_op jit(solution)/shard_map/ppermute | solution.py:373
